TPU v7x, 128 devices: a whole 4x4x4 slice. The times are simulated.
128 devices in a mesh: seg: 32 (over x_lo, z, y), pair: 4 (over x_hi, core).
Axes of the slice: x: 4 (x_hi: 2, x_lo: 2; x = x_hi * 2 + x_lo), y: 4, z: 4, core: 2. Of those that a mesh axis runs over, the one named last changes fastest.
Arguments:
- embeddings: bfloat16 [98304, 768], P(('seg', 'pair')), may hold values from -60 to 60
- cluster_id: int32 [98304], P(('seg', 'pair')), may hold values from 0 to 127, as said below
- cluster_rank: int32 [98304], P(('seg', 'pair')), may hold values from 0 to 2687, as said below
- dest_slot: int32 [98304], P(('seg', 'pair')), may hold values from 0 to 98303, as said below
Outputs:
- best_all: float32 [98304], P(('seg', 'pair'))
- best_higher: float32 [98304], P(('seg', 'pair'))
Inputs may be any that keep to these rules, and one draw needn't show every extreme that they name: `cluster_id`: rows of one cluster share an id, distinct clusters have distinct ids, and a cluster fills 192 to 2688 consecutive cycle positions (dest_slot, modulo 98304); clusters of both sizes occur. `cluster_rank`: within each cluster the ranks are 0 to its size - 1, each once. `dest_slot`: a permutation of the rows onto cycle positions; the device with seg index a and pair index b holds storage rows a * 4 + b and owns cycle positions (a * 4 + b) * 768 to (a * 4 + b + 1) * 768 - 1; each device's rows fall on at most 9 positions owned by any one device, and on exactly 9 of some device's.
All inputs are finite; a program needn't handle non-finite values.
Results may differ from a plain program's by a relative error of at most 0.00051.
Values may be sent and summed in bfloat16 or wider, within the bound.
No kernel may reach another device: no remote copies, remote signals or barrier semaphores. Data moves between devices by JAX's collectives and lax.ppermute only.
A program may use at most 128 MiB of HBM per device.

v0:
```python
import jax
import jax.numpy as jnp
from jax import lax
from jax.experimental import pallas as pl
from jax.experimental.pallas import tpu as pltpu
from jax.sharding import PartitionSpec as P

AXES = ("seg", "pair")
DEVICES = 128
CHIPS = 64
ROWS = 768
HALF = 384
CAP = 9
SLOTS = DEVICES * CAP
MAIN = DEVICES * 8
META = 16
ROLES = 5
BF = jnp.bfloat16
F32 = jnp.float32
NT = (((1,), (1,)), ((), ()))


def device_of(block):
    block = block & (DEVICES - 1)
    chip, core = block >> 1, block & 1
    high, mid, low = chip >> 4, (chip >> 2) & 3, chip & 3
    x, y, z = (mid - high) & 3, (low - mid) & 3, high
    return ((((x & 1) * 4 + z) * 4 + y) << 2) + ((x >> 1) << 1) + core


def routes(source_of, targets):
    return [(device_of(source_of(t)), device_of(t)) for t in targets]


def iota(shape, dim):
    return lax.broadcasted_iota(jnp.int32, shape, dim)


def dot(a, b):
    return jnp.dot(a, b, preferred_element_type=F32)


def dot_nt(a, b):
    return lax.dot_general(a, b, NT, preferred_element_type=F32)


def split_slot(slot):
    block = ((slot >> 8) * 171) >> 9
    return block, slot - block * ROWS


def place(slot):
    block, local = split_slot(slot)
    device = device_of(block)
    to_device = (iota((DEVICES, ROWS), 0) == device).astype(BF)
    earlier = (iota((ROWS, ROWS), 0) < iota((ROWS, ROWS), 1)).astype(BF)
    before = dot(to_device, earlier)
    within = jnp.sum(to_device.astype(F32) * before, axis=0, keepdims=True).astype(jnp.int32)
    return block, device, local, within, to_device


def pack_kernel(emb_ref, cid_ref, rank_ref, slot_ref, out_ref, unit, extra):
    values = emb_ref[...].astype(F32)
    scaling = lax.rsqrt(jnp.sum(values * values, axis=1, keepdims=True) + 1e-06)
    unit[...] = (values * scaling).astype(BF)
    _, device, local, within, to_device = place(slot_ref[...])
    flat = jnp.where(within < 8, device * 8 + within, -1)
    for start in range(0, MAIN, 256):
        pick = (iota((256, ROWS), 0) + start == flat).astype(BF)
        out_ref[start : start + 256, :ROWS] = dot(pick, unit[...]).astype(BF)
    ninth = jnp.where(within == 8, to_device, jnp.zeros_like(to_device))
    ninth_rows = dot(ninth, unit[...])
    field = iota((DEVICES, ROWS), 0) >> 4
    cid, rank = cid_ref[...], rank_ref[...]
    meta = jnp.where(field == 0, (local >> 8) + 1, jnp.where(field == 1, local & 255, jnp.where(field == 2, cid + 1, 0)))
    meta = jnp.where(field == 3, rank >> 8, jnp.where(field == 4, rank & 255, meta))
    meta = jnp.where((iota((DEVICES, ROWS), 0) & 15) == within, meta, 0).astype(F32).astype(BF)
    extra[...] = jnp.zeros_like(extra)
    for part in range(6):
        extra[pl.ds(part, DEVICES, stride=8), :] = ninth_rows[:, part * 128 : (part + 1) * 128]
    extra[pl.ds(6, DEVICES, stride=8), :] = dot_nt(to_device, meta)
    out_ref[:, ROWS:] = extra[...].astype(BF)


def unpack_kernel(got_ref, out_ref, extra, spread):
    extra[...] = got_ref[:, ROWS:].astype(F32)
    ninth_rows = jnp.concatenate([extra[pl.ds(part, DEVICES, stride=8), :] for part in range(6)], axis=1).astype(BF)
    meta = extra[pl.ds(6, DEVICES, stride=8), :]
    for order in range(8):
        spread[pl.ds(order, DEVICES, stride=8), :] = meta
    lane, row = iota((MAIN, 128), 1), iota((MAIN, 128), 0)
    main = jnp.where((lane & 15) == (row & 7), spread[...], 0.0).astype(BF)
    last = jnp.where((iota((DEVICES, 128), 1) & 15) == 8, meta, 0.0).astype(BF)
    fields = ((iota((META, 128), 1) >> 4) == iota((META, 128), 0)).astype(BF)
    by_slot = jnp.concatenate([dot_nt(fields, main), dot_nt(fields, last)], axis=1)
    slot = ((by_slot[0:1] - 1.0) * 256.0 + by_slot[1:2]).astype(jnp.int32)
    cols = by_slot.astype(BF)
    for start in range(0, ROWS, 256):
        pick = (iota((256, SLOTS), 0) + start == slot).astype(BF)
        rows = dot(pick[:, :MAIN], got_ref[:, :ROWS]) + dot(pick[:, MAIN:], ninth_rows)
        out_ref[start : start + 256, :] = rows.astype(BF)
        placed = dot_nt(cols, pick)
        kept = jnp.concatenate([placed[2:5], jnp.zeros((13, 256), F32)], axis=0)
        out_ref[ROWS:, start : start + 256] = kept.astype(BF)
    out_ref[ROWS + 8 : ROWS + 9, :] = cols[0:1, :ROWS]
    out_ref[ROWS + 9 : ROWS + 10, :] = cols[1:2, :ROWS]
    out_ref[ROWS + 10 : ROWS + 11, :HALF] = cols[0:1, ROWS:]
    out_ref[ROWS + 11 : ROWS + 12, :HALF] = cols[1:2, ROWS:]


def read_meta(block_ref, rows):
    meta = block_ref[rows:, :].astype(F32)
    cid, rank = meta[0:1], meta[1:2] * 256.0 + meta[2:3]
    high = jnp.concatenate([meta[8:9], meta[10:11, :HALF]], axis=1)
    low = jnp.concatenate([meta[9:10], meta[11:12, :HALF]], axis=1)
    slot = ((high - 1.0) * 256.0 + low).astype(jnp.int32)
    return cid, rank, slot


def columns(cid, rank):
    both = jnp.concatenate([cid, rank, jnp.zeros((6, ROWS), F32)], axis=0)
    turned = jnp.transpose(both)
    return turned[:, 0:1], turned[:, 1:2]


def local_kernel(own_ref, other_ref, out_ref):
    own_cid, own_rank, _ = read_meta(own_ref, ROWS)
    best_all = jnp.full((8, ROWS), -1.0, F32)
    best_high = jnp.full((8, ROWS), -1.0, F32)
    for ref in (own_ref, other_ref):
        cid, rank, _ = read_meta(ref, ROWS)
        cid, rank = columns(cid, rank)
        for start in range(0, ROWS, 256):
            cosine = dot_nt(ref[start : start + 256, :], own_ref[:ROWS, :])
            c, r = cid[start : start + 256], rank[start : start + 256]
            near = jnp.where((c == own_cid) & (r != own_rank), cosine, -1.0)
            high = jnp.where(r < own_rank, near, -1.0)
            best_all = jnp.maximum(best_all, jnp.max(near.reshape(32, 8, ROWS), axis=0))
            best_high = jnp.maximum(best_high, jnp.max(high.reshape(32, 8, ROWS), axis=0))
    out_ref[0:1, :] = jnp.max(best_all, axis=0, keepdims=True)
    out_ref[1:2, :] = jnp.max(best_high, axis=0, keepdims=True)
    out_ref[2:, :] = jnp.full((6, ROWS), -1.0, F32)


def against(key_ref, rows, key_cid, key_rank, other_ref, first, count, other_cid, other_rank):
    key_all, key_high = [], []
    best_all = jnp.full((8, count), -1.0, F32)
    best_high = jnp.full((8, count), -1.0, F32)
    for start in range(0, rows, 128):
        cosine = dot_nt(key_ref[start : start + 128, :], other_ref[first : first + count, :])
        near = jnp.where(key_cid[start : start + 128] == other_cid, cosine, -1.0)
        before = other_rank < key_rank[start : start + 128]
        high = jnp.where(before, near, -1.0)
        low = jnp.where(before, -1.0, near)
        best_all = jnp.maximum(best_all, jnp.max(near.reshape(16, 8, count), axis=0))
        best_high = jnp.maximum(best_high, jnp.max(low.reshape(16, 8, count), axis=0))
        wide_all, wide_high = near[:, :128], high[:, :128]
        for lane in range(128, count, 128):
            wide_all = jnp.maximum(wide_all, near[:, lane : lane + 128])
            wide_high = jnp.maximum(wide_high, high[:, lane : lane + 128])
        key_all.append(wide_all)
        key_high.append(wide_high)
    best_all = jnp.max(best_all, axis=0, keepdims=True)
    best_high = jnp.max(best_high, axis=0, keepdims=True)
    return jnp.concatenate(key_all, axis=0), jnp.concatenate(key_high, axis=0), best_all, best_high


def far_kernel(key_ref, own_ref, other_ref, prev_ref, tail_ref, local_ref, out_ref, by_slot):
    key_cid, key_rank, key_slot = read_meta(key_ref, ROWS)
    cid_col, rank_col = columns(key_cid, key_rank)
    key_all = jnp.full((ROWS, 128), -1.0, F32)
    key_high = jnp.full((ROWS, 128), -1.0, F32)
    found = []
    for ref in (own_ref, other_ref, prev_ref):
        cid, rank, slot = read_meta(ref, ROWS)
        wide_all, wide_high, best_all, best_high = against(key_ref, ROWS, cid_col, rank_col, ref, 0, ROWS, cid, rank)
        key_all = jnp.maximum(key_all, wide_all)
        key_high = jnp.maximum(key_high, wide_high)
        found.append((best_all, best_high, slot))
    cid, rank, slot = read_meta(tail_ref, HALF)
    wide_all, wide_high, best_all, best_high = against(
        key_ref, HALF, cid_col, rank_col, tail_ref, 0, HALF, cid[:, HALF:], rank[:, HALF:]
    )
    key_all = jnp.concatenate([jnp.maximum(key_all[:HALF], wide_all), key_all[HALF:]], axis=0)
    key_high = jnp.concatenate([jnp.maximum(key_high[:HALF], wide_high), key_high[HALF:]], axis=0)
    key_all = jnp.max(jnp.transpose(key_all), axis=0, keepdims=True)
    key_high = jnp.max(jnp.transpose(key_high), axis=0, keepdims=True)
    own_all = jnp.maximum(found[0][0], local_ref[0:1, :])
    own_high = jnp.maximum(found[0][1], local_ref[1:2, :])
    parts = [
        (own_all, own_high, found[0][2]),
        found[1],
        (key_all, key_high, key_slot),
        found[2],
        (best_all, best_high, slot - HALF),
    ]
    total = jnp.zeros((128, SLOTS), F32)
    for role, (value_all, value_high, slot) in enumerate(parts):
        count = value_all.shape[1]
        pick = (iota((count, SLOTS), 0) == slot).astype(BF)
        stacked = jnp.zeros((128, count), F32)
        row = iota((128, count), 0)
        for which, value in enumerate((value_all, value_high)):
            rest = value
            for piece in range(3):
                rounded = rest.astype(BF).astype(F32)
                rest = rest - rounded
                stacked = jnp.where(row == piece * 32 + role * 2 + which, rounded, stacked)
        total = total + dot(stacked.astype(BF), pick)
    total = total[0:32] + total[32:64] + total[64:96]
    total = jnp.concatenate([total, jnp.zeros((96, SLOTS), F32)], axis=0)
    by_slot[...] = jnp.transpose(total)
    reply = by_slot[pl.ds(0, DEVICES, stride=8), :]
    for order in range(1, 8):
        reply = reply + pltpu.roll(by_slot[pl.ds(order, DEVICES, stride=8), :], order * 2 * ROLES, 1)
    reply = reply + pltpu.roll(by_slot[MAIN:, :], 16 * ROLES, 1)
    out_ref[...] = reply


def answer_kernel(got_ref, slot_ref, out_ref):
    block, device, local, within, _ = place(slot_ref[...])
    replies = jnp.transpose(got_ref[...])
    pieces = []
    rest = replies
    for piece in range(3):
        rounded = rest.astype(BF)
        pieces.append(rounded)
        rest = rest - rounded.astype(F32)
    pieces = jnp.concatenate(pieces, axis=1)
    senders = (device, device_of(block ^ 1), device_of(block - 2), device_of(block + 1), device_of(block + 2))
    valid = (None, None, None, (block & 1) == 1, local >= HALF)
    lane = iota((128, ROWS), 0)
    result = [None, None]
    for role in range(ROLES):
        sent = (iota((DEVICES, ROWS), 0) == senders[role]).astype(BF)
        lines = dot(pieces, jnp.concatenate([sent, sent, sent], axis=0))
        for which in range(2):
            mine = jnp.where(lane == within * (2 * ROLES) + role * 2 + which, lines, 0.0)
            value = jnp.sum(mine, axis=0, keepdims=True)
            if valid[role] is not None:
                value = jnp.where(valid[role], value, -1.0)
            result[which] = value if result[which] is None else jnp.maximum(result[which], value)
    out_ref[...] = jnp.concatenate([result[0], result[1], jnp.zeros((6, ROWS), F32)], axis=0)


def call(kernel, out, args, scratch=(), flops=0, name=None):
    moved = sum(a.size * a.dtype.itemsize for a in args)
    return pl.pallas_call(
        kernel,
        out_shape=jax.ShapeDtypeStruct(*out),
        in_specs=[pl.BlockSpec(memory_space=pltpu.VMEM)] * len(args),
        out_specs=pl.BlockSpec(memory_space=pltpu.VMEM),
        scratch_shapes=list(scratch),
        compiler_params=pltpu.CompilerParams(vmem_limit_bytes=48 * 1024 * 1024),
        cost_estimate=pl.CostEstimate(flops=flops, bytes_accessed=moved, transcendentals=0),
        name=name,
    )(*args)


def body(embeddings, cluster_id, cluster_rank, dest_slot):
    cid, rank, slot = (a.reshape(1, ROWS) for a in (cluster_id, cluster_rank, dest_slot))
    send = call(
        pack_kernel,
        ((MAIN, ROWS + 128), BF),
        (embeddings, cid, rank, slot),
        (pltpu.VMEM((ROWS, ROWS), BF), pltpu.VMEM((MAIN, 128), F32)),
        name="pack",
    )
    got = lax.all_to_all(send, AXES, split_axis=0, concat_axis=0, tiled=True)
    own = call(
        unpack_kernel,
        ((ROWS + META, ROWS), BF),
        (got,),
        (pltpu.VMEM((MAIN, 128), F32), pltpu.VMEM((MAIN, 128), F32)),
        name="unpack",
    )
    everyone = range(DEVICES)
    other = lax.ppermute(own, AXES, routes(lambda t: t ^ 1, everyone))
    key = lax.ppermute(own, AXES, routes(lambda t: t + 2, everyone))
    prev = lax.ppermute(own, AXES, routes(lambda t: t - 1, range(0, DEVICES, 2)))
    tail = lax.ppermute(own[HALF:], AXES, routes(lambda t: t - 2, everyone))
    tile = 2 * ROWS**3
    local = call(local_kernel, ((8, ROWS), F32), (own, other), flops=2 * tile, name="local")
    reply = call(
        far_kernel,
        ((DEVICES, 128), F32),
        (key, own, other, prev, tail, local),
        (pltpu.VMEM((SLOTS, 128), F32),),
        flops=4 * tile,
        name="far",
    )
    answer = lax.all_to_all(reply.reshape(DEVICES, 1, 128), AXES, split_axis=0, concat_axis=0, tiled=True)
    out = call(answer_kernel, ((8, ROWS), F32), (answer.reshape(DEVICES, 128), slot), name="answer")
    return out[0], out[1]


def solution(mesh):
    rows = P(AXES)
    return jax.shard_map(
        body,
        mesh=mesh,
        in_specs=(P(AXES, None), rows, rows, rows),
        out_specs=(rows, rows),
        check_vma=False,
    )
```

profile of v0, /device:TPU:1, one launch (start us, length us, event | category | flops | bytes accessed | tf_op | source)
XLA Modules:
  0.0 104.7 jit_solution(10054648736849672999)
XLA Ops:
  0.6 0.7 reshape.23.slot_ref
  1.3 0.7 reshape.21.cid_ref
  2.0 0.7 reshape.22.rank_ref
  2.7 0.0 copy-start
  2.7 1.3 %copy-done = bf16[768,768]{1,0:T(8,128)(2,1)S(1)} copy-done((bf16[768,768]{1,0:T(8,128)(2,1)S(1)}, bf16[768,768]{1,0:T(8,128)(2,1)}, u32[]{:S(2)}) %copy-start) | copy-done | bytes 1179672
  4.0 2.2 %pack.1 = bf16[1024,896]{1,0:T(8,128)(2,1)S(1)} custom-call(bf16[768,768]{1,0:T(8,128)(2,1)S(1)} %copy-done, s32[1,768]{1,0:T(1,128)S(1)} %reshape.21.cid_ref, s32[1,768]{1,0:T(1,128)S(1)} %reshape.22.rank_ref, s32[1,768]{1,0:T(1,128)S(1)} %reshape.23.slot_ref), custom_call_target="tpu_custom_call" | custom-call | bytes 1188864 | tf_op jit(solution)/shard_map/pack/pallas_call | solution.py:248
  6.2 38.8 %all_to_all.16 = bf16[128,8,896]{2,1,0:T(8,128)(2,1)S(1)} all-to-all(bf16[128,8,896]{2,1,0:T(8,128)(2,1)S(1)} %bitcast.6), channel_id=1, replica_groups=mesh['seg'=32,'pair'=4] {'seg','pair'}, dimensions={0} | all-to-all | bytes 3670016 | tf_op jit(solution)/shard_map/all_to_all | solution.py:269
  45.0 2.3 %unpack.1.own_ref = bf16[784,768]{1,0:T(8,128)(2,1)S(1)} custom-call(bf16[1024,896]{1,0:T(8,128)(2,1)S(1)} %bitcast.7), custom_call_target="tpu_custom_call" | custom-call | bytes 1835008 | tf_op jit(solution)/shard_map/unpack/pallas_call | solution.py:248
  47.3 0.1 collective-permute-start.1
  47.4 1.4 %collective-permute-start.2 = (bf16[784,768]{1,0:T(8,128)(2,1)S(1)}, bf16[784,768]{1,0:T(8,128)(2,1)S(1)}, u32[]{:S(2)}, u32[]{:S(2)}) collective-permute-start(bf16[784,768]{1,0:T(8,128)(2,1)S(1)} %unpack.1.own_ref), channel_id=1, source_target_pairs={{49,0},{1,4},{5,8},{9,12},{13,76},{77,64},{65,68},{69,72},{73,10},... | collective-permute-start | bytes 3612680 | tf_op jit(solution)/shard_map/ppermute | solution.py:280
  48.8 3.7 %collective-permute-start = (bf16[784,768]{1,0:T(8,128)(2,1)S(1)}, bf16[784,768]{1,0:T(8,128)(2,1)S(1)}, u32[]{:S(2)}, u32[]{:S(2)}) collective-permute-start(bf16[784,768]{1,0:T(8,128)(2,1)S(1)} %unpack.1.own_ref), channel_id=1, source_target_pairs={{4,0},{5,1},{8,4},{9,5},{12,8},{13,9},{76,12},{77,13},{64,76},{65,... | collective-permute-start | bytes 3612680 | tf_op jit(solution)/shard_map/ppermute | solution.py:279
  52.6 0.3 collective-permute-start.3
  52.8 0.0 collective-permute-done.1.other_ref
  52.8 2.5 %local.1.local_ref = f32[8,768]{1,0:T(8,128)S(1)} custom-call(bf16[784,768]{1,0:T(8,128)(2,1)S(1)} %unpack.1.own_ref, bf16[784,768]{1,0:T(8,128)(2,1)S(1)} %collective-permute-done.1.other_ref), custom_call_target="tpu_custom_call" | custom-call | flops 1811939328 | bytes 2408448 | tf_op jit(solution)/shard_map/local/pallas_call | solution.py:248
  55.4 24.0 %collective-permute-done.3.tail_ref = bf16[400,768]{1,0:T(8,128)(2,1)S(1)} collective-permute-done((bf16[400,768]{1,0:T(8,128)(2,1)S(1)}, bf16[400,768]{1,0:T(8,128)(2,1)S(1)}, u32[]{:S(2)}, u32[]{:S(2)}) %collective-permute-start.3) | collective-permute-done | bytes 614432 | tf_op jit(solution)/shard_map/ppermute | solution.py:281
  79.4 0.0 collective-permute-done.2.prev_ref
  79.4 0.0 collective-permute-done.key_ref
  79.4 10.3 %far.1 = f32[128,128]{1,0:T(8,128)S(1)} custom-call(bf16[784,768]{1,0:T(8,128)(2,1)S(1)} %collective-permute-done.key_ref, bf16[784,768]{1,0:T(8,128)(2,1)S(1)} %unpack.1.own_ref, bf16[784,768]{1,0:T(8,128)(2,1)S(1)} %collective-permute-done.1.other_ref, bf16[784,768]{1,0:T(8,128)(2,1)S(1)} %collective-permute-done.2.prev_ref, ...), custom_call_target="tpu_custom_call" | custom-call | flops 3623878656 | bytes 5455872 | tf_op jit(solution)/shard_map/far/pallas_call | solution.py:248
  89.7 13.1 %all_to_all.17 = f32[128,1,128]{2,1,0:T(1,128)S(1)} all-to-all(f32[128,1,128]{2,1,0:T(1,128)S(1)} %bitcast.9), channel_id=1, replica_groups=mesh['seg'=32,'pair'=4] {'seg','pair'}, dimensions={0} | all-to-all | bytes 131072 | tf_op jit(solution)/shard_map/all_to_all | solution.py:292
  102.8 1.3 %answer.1 = f32[8,768]{1,0:T(8,128)S(1)} custom-call(f32[128,128]{1,0:T(8,128)S(1)} %bitcast.8, s32[1,768]{1,0:T(1,128)S(1)} %reshape.23.slot_ref), custom_call_target="tpu_custom_call" | custom-call | bytes 68608 | tf_op jit(solution)/shard_map/answer/pallas_call | solution.py:248
  104.0 0.6 slice_reduce_fusion
  (1 shorter events, 0.0 us)
Async XLA Ops:
  2.7 1.3 %copy-start = (bf16[768,768]{1,0:T(8,128)(2,1)S(1)}, bf16[768,768]{1,0:T(8,128)(2,1)}, u32[]{:S(2)}) copy-start(bf16[768,768]{1,0:T(8,128)(2,1)} %emb_ref.1) | copy-start | bytes 3538948
  47.3 5.5 %collective-permute-start.1 = (bf16[784,768]{1,0:T(8,128)(2,1)S(1)}, bf16[784,768]{1,0:T(8,128)(2,1)S(1)}, u32[]{:S(2)}, u32[]{:S(2)}) collective-permute-start(bf16[784,768]{1,0:T(8,128)(2,1)S(1)} %unpack.1.own_ref), channel_id=1, source_target_pairs={{1,0},{0,1},{5,4},{4,5},{9,8},{8,9},{13,12},{12,13},{77,76},{76,77... | collective-permute-start | bytes 3612680 | tf_op jit(solution)/shard_map/ppermute | solution.py:278
  47.4 32.0 %collective-permute-start.2 = (bf16[784,768]{1,0:T(8,128)(2,1)S(1)}, bf16[784,768]{1,0:T(8,128)(2,1)S(1)}, u32[]{:S(2)}, u32[]{:S(2)}) collective-permute-start(bf16[784,768]{1,0:T(8,128)(2,1)S(1)} %unpack.1.own_ref), channel_id=1, source_target_pairs={{49,0},{1,4},{5,8},{9,12},{13,76},{77,64},{65,68},{69,72},{73,10},... | collective-permute-start | bytes 3612680 | tf_op jit(solution)/shard_map/ppermute | solution.py:280
  48.8 30.6 %collective-permute-start = (bf16[784,768]{1,0:T(8,128)(2,1)S(1)}, bf16[784,768]{1,0:T(8,128)(2,1)S(1)}, u32[]{:S(2)}, u32[]{:S(2)}) collective-permute-start(bf16[784,768]{1,0:T(8,128)(2,1)S(1)} %unpack.1.own_ref), channel_id=1, source_target_pairs={{4,0},{5,1},{8,4},{9,5},{12,8},{13,9},{76,12},{77,13},{64,76},{65,... | collective-permute-start | bytes 3612680 | tf_op jit(solution)/shard_map/ppermute | solution.py:279
  52.6 26.8 %collective-permute-start.3 = (bf16[400,768]{1,0:T(8,128)(2,1)S(1)}, bf16[400,768]{1,0:T(8,128)(2,1)S(1)}, u32[]{:S(2)}, u32[]{:S(2)}) collective-permute-start(bf16[400,768]{1,0:T(8,128)(2,1)S(1)} %slice.12), channel_id=1, source_target_pairs={{48,0},{49,1},{0,4},{1,5},{4,8},{5,9},{8,12},{9,13},{12,76},{13,77... | collective-permute-start | bytes 1843208 | tf_op jit(solution)/shard_map/ppermute | solution.py:281
where the time goes:
time: 105 us
  blocking collectives  51.9 us (49%)
  waiting for transfers between devices  24 us (23%)
  Pallas kernels  18.6 us (18%)
  starting transfers between devices  5.44 us (5%)
  local copies, waits for them, and re-layouts  3.99 us (4%)
    all_to_all x1, blocking collectives, body(): got = lax.all_to_all(send, AXES, split_axis=0, concat_axis=0, tiled=True)  38.8 us
    ppermute x1, waiting for transfers between devices, body(): tail = lax.ppermute(own[HALF:], AXES, routes(lambda t: t - 2, everyone))  24 us
    pallas_call x5, Pallas kernels, call(): pl.pallas_call(kernel, out_shape=jax.ShapeDtypeStruct(*out), in_specs=[pl...  18.6 us
    all_to_all x1, blocking collectives, body(): lax.all_to_all(reply.reshape(DEVICES, 1, 128), AXES, split_axis=0, concat...  13.1 us
    ppermute x1, starting transfers between devices, body(): key = lax.ppermute(own, AXES, routes(lambda t: t + 2, everyone))  3.73 us
  transfers between devices with their start and end apart: 4, of which 1 were waited for; matrix products, arithmetic and copies ran while one was open for 0% of the time, Pallas kernels for 2%

commit v1 on v0

v1 whole, which is shorter than its diff:
```python
import jax
import jax.numpy as jnp
from jax import lax
from jax.experimental import pallas as pl
from jax.experimental.pallas import tpu as pltpu
from jax.sharding import PartitionSpec as P

AXES = ("seg", "pair")
DEVICES = 128
CHIPS = [
    (2, 0, 1), (2, 1, 1), (2, 1, 2), (2, 1, 3), (2, 2, 3), (1, 2, 3), (1, 2, 0), (0, 2, 0),
    (0, 1, 0), (0, 1, 1), (1, 1, 1), (1, 2, 1), (2, 2, 1), (2, 2, 0), (2, 1, 0), (1, 1, 0),
    (1, 1, 3), (0, 1, 3), (3, 1, 3), (3, 1, 2), (0, 1, 2), (0, 0, 2), (0, 0, 3), (0, 0, 0),
    (1, 0, 0), (2, 0, 0), (2, 0, 3), (3, 0, 3), (3, 3, 3), (3, 2, 3), (3, 2, 0), (3, 2, 1),
    (3, 1, 1), (3, 1, 0), (3, 0, 0), (3, 3, 0), (3, 3, 1), (2, 3, 1), (1, 3, 1), (1, 0, 1),
    (0, 0, 1), (0, 3, 1), (0, 2, 1), (0, 2, 2), (0, 2, 3), (0, 3, 3), (0, 3, 0), (1, 3, 0),
    (2, 3, 0), (2, 3, 3), (1, 3, 3), (1, 0, 3), (1, 0, 2), (1, 1, 2), (1, 2, 2), (1, 3, 2),
    (0, 3, 2), (3, 3, 2), (3, 2, 2), (2, 2, 2), (2, 3, 2), (2, 0, 2), (3, 0, 2), (3, 0, 1),
]
ROWS = 768
HALF = 384
CAP = 9
SLOTS = DEVICES * CAP
MAIN = DEVICES * 8
META = 16
ROLES = 5
BF = jnp.bfloat16
F32 = jnp.float32
NT = (((1,), (1,)), ((), ()))


def chip_device(x, y, z):
    return ((((x & 1) * 4 + z) * 4 + y) << 2) + ((x >> 1) << 1)


WALK = [chip_device(*chip) for chip in CHIPS]


def device_of(block):
    block = block % DEVICES
    return WALK[block >> 1] + (block & 1)


def routes(source_of, targets):
    return [(device_of(source_of(t)), device_of(t)) for t in targets]


def iota(shape, dim):
    return lax.broadcasted_iota(jnp.int32, shape, dim)


def dot(a, b):
    return jnp.dot(a, b, preferred_element_type=F32)


def dot_nt(a, b):
    return lax.dot_general(a, b, NT, preferred_element_type=F32)


def split_slot(slot):
    block = ((slot >> 8) * 171) >> 9
    return block, slot - block * ROWS


def device_table():
    row, lane = iota((8, DEVICES), 0), iota((8, DEVICES), 1)
    step = jnp.where(row == 2, -2, jnp.where(row == 3, 1, jnp.where(row == 4, 2, 0)))
    block = jnp.where(row == 1, lane ^ 1, lane + step) & (DEVICES - 1)
    chip = block >> 1
    found = block & 1
    for index, device in enumerate(WALK):
        found = found + jnp.where(chip == index, device, 0)
    return found.astype(F32).astype(BF)


def pack_kernel(emb_ref, cid_ref, rank_ref, slot_ref, out_ref, route_ref, raw, slots, cids, ranks, unit, extra, sems):
    ids = ((slot_ref, slots), (cid_ref, cids), (rank_ref, ranks))
    small = [pltpu.make_async_copy(*pair, sems.at[3 + i]) for i, pair in enumerate(ids)]
    copies = [
        pltpu.make_async_copy(emb_ref.at[pl.ds(part * 256, 256)], raw.at[pl.ds(part * 256, 256)], sems.at[part])
        for part in range(3)
    ]
    for copy in small + copies:
        copy.start()
    table = device_table()
    earlier = (iota((ROWS, ROWS), 0) < iota((ROWS, ROWS), 1)).astype(BF)
    for copy in small:
        copy.wait()
    slot, cid, rank = (ref[...].reshape(1, ROWS) for _, ref in ids)
    block, local = split_slot(slot)
    to_block = (iota((DEVICES, ROWS), 0) == block).astype(BF)
    within = jnp.sum(to_block.astype(F32) * dot(to_block, earlier), axis=0, keepdims=True).astype(jnp.int32)
    senders = dot(table, to_block).astype(jnp.int32)
    row = iota((8, ROWS), 0)
    dropped = ((row == 3) & ((block & 1) == 0)) | ((row == 4) & (local < HALF))
    route_ref[...] = jnp.where(row == 5, within, jnp.where(dropped, -1, senders))
    device = senders[0:1]
    to_device = (iota((DEVICES, ROWS), 0) == device).astype(BF)
    flat = jnp.where(within < 8, device * 8 + within, -1)
    for part, copy in enumerate(copies):
        copy.wait()
        values = raw[part * 256 : (part + 1) * 256, :].astype(F32)
        scaling = lax.rsqrt(jnp.sum(values * values, axis=1, keepdims=True) + 1e-06)
        unit[part * 256 : (part + 1) * 256, :] = (values * scaling).astype(BF)
    for start in range(0, MAIN, 256):
        pick = (iota((256, ROWS), 0) + start == flat).astype(BF)
        out_ref[start : start + 256, :ROWS] = dot(pick, unit[...]).astype(BF)
    ninth = jnp.where(within == 8, to_device, jnp.zeros_like(to_device))
    ninth_rows = dot(ninth, unit[...])
    field = iota((DEVICES, ROWS), 0) >> 4
    meta = jnp.where(field == 0, (local >> 8) + 1, jnp.where(field == 1, local & 255, jnp.where(field == 2, cid + 1, 0)))
    meta = jnp.where(field == 3, rank >> 8, jnp.where(field == 4, rank & 255, meta))
    meta = jnp.where((iota((DEVICES, ROWS), 0) & 15) == within, meta, 0).astype(F32).astype(BF)
    extra[...] = jnp.zeros_like(extra)
    for part in range(6):
        extra[pl.ds(part, DEVICES, stride=8), :] = ninth_rows[:, part * 128 : (part + 1) * 128]
    extra[pl.ds(6, DEVICES, stride=8), :] = dot_nt(to_device, meta)
    out_ref[:, ROWS:] = extra[...].astype(BF)


def unpack_kernel(got_ref, out_ref, extra, spread):
    extra[...] = got_ref[:, ROWS:].astype(F32)
    ninth_rows = jnp.concatenate([extra[pl.ds(part, DEVICES, stride=8), :] for part in range(6)], axis=1).astype(BF)
    meta = extra[pl.ds(6, DEVICES, stride=8), :]
    for order in range(8):
        spread[pl.ds(order, DEVICES, stride=8), :] = meta
    lane, row = iota((MAIN, 128), 1), iota((MAIN, 128), 0)
    main = jnp.where((lane & 15) == (row & 7), spread[...], 0.0).astype(BF)
    last = jnp.where((iota((DEVICES, 128), 1) & 15) == 8, meta, 0.0).astype(BF)
    fields = ((iota((META, 128), 1) >> 4) == iota((META, 128), 0)).astype(BF)
    by_slot = jnp.concatenate([dot_nt(fields, main), dot_nt(fields, last)], axis=1)
    slot = ((by_slot[0:1] - 1.0) * 256.0 + by_slot[1:2]).astype(jnp.int32)
    cols = by_slot.astype(BF)
    for start in range(0, ROWS, 256):
        pick = (iota((256, SLOTS), 0) + start == slot).astype(BF)
        rows = dot(pick[:, :MAIN], got_ref[:, :ROWS]) + dot(pick[:, MAIN:], ninth_rows)
        out_ref[start : start + 256, :] = rows.astype(BF)
        placed = dot_nt(cols, pick)
        kept = jnp.concatenate([placed[2:5], jnp.zeros((13, 256), F32)], axis=0)
        out_ref[ROWS:, start : start + 256] = kept.astype(BF)
    out_ref[ROWS + 8 : ROWS + 9, :] = cols[0:1, :ROWS]
    out_ref[ROWS + 9 : ROWS + 10, :] = cols[1:2, :ROWS]
    out_ref[ROWS + 10 : ROWS + 11, :HALF] = cols[0:1, ROWS:]
    out_ref[ROWS + 11 : ROWS + 12, :HALF] = cols[1:2, ROWS:]


def read_meta(block_ref, rows):
    meta = block_ref[rows:, :].astype(F32)
    cid, rank = meta[0:1], meta[1:2] * 256.0 + meta[2:3]
    high = jnp.concatenate([meta[8:9], meta[10:11, :HALF]], axis=1)
    low = jnp.concatenate([meta[9:10], meta[11:12, :HALF]], axis=1)
    slot = ((high - 1.0) * 256.0 + low).astype(jnp.int32)
    return cid, rank, slot


def columns(cid, rank):
    both = jnp.concatenate([cid, rank, jnp.zeros((6, ROWS), F32)], axis=0)
    turned = jnp.transpose(both)
    return turned[:, 0:1], turned[:, 1:2]


def local_kernel(own_ref, other_ref, out_ref):
    own_cid, own_rank, _ = read_meta(own_ref, ROWS)
    best_all = jnp.full((8, ROWS), -1.0, F32)
    best_high = jnp.full((8, ROWS), -1.0, F32)
    for ref in (own_ref, other_ref):
        cid, rank, _ = read_meta(ref, ROWS)
        cid, rank = columns(cid, rank)
        for start in range(0, ROWS, 256):
            cosine = dot_nt(ref[start : start + 256, :], own_ref[:ROWS, :])
            c, r = cid[start : start + 256], rank[start : start + 256]
            near = jnp.where((c == own_cid) & (r != own_rank), cosine, -1.0)
            high = jnp.where(r < own_rank, near, -1.0)
            best_all = jnp.maximum(best_all, jnp.max(near.reshape(32, 8, ROWS), axis=0))
            best_high = jnp.maximum(best_high, jnp.max(high.reshape(32, 8, ROWS), axis=0))
    out_ref[0:1, :] = jnp.max(best_all, axis=0, keepdims=True)
    out_ref[1:2, :] = jnp.max(best_high, axis=0, keepdims=True)
    out_ref[2:, :] = jnp.full((6, ROWS), -1.0, F32)


def against(key, key_cid, key_rank, other_ref, count, other_cid, other_rank):
    cosine = dot_nt(key, other_ref[:count, :])
    near = jnp.where(key_cid == other_cid, cosine, -1.0)
    before = other_rank < key_rank
    high = jnp.where(before, near, -1.0)
    low = jnp.where(before, -1.0, near)
    wide_all, wide_high = near[:, :128], high[:, :128]
    for lane in range(128, count, 128):
        wide_all = jnp.maximum(wide_all, near[:, lane : lane + 128])
        wide_high = jnp.maximum(wide_high, high[:, lane : lane + 128])
    return wide_all, wide_high, jnp.max(near, axis=0, keepdims=True), jnp.max(low, axis=0, keepdims=True)


def reply_rows(value, slot):
    groups = value.shape[1] // 128
    rows = [value[:, g * 128 : (g + 1) * 128] for g in range(groups)]
    rest = jnp.concatenate(rows + [jnp.zeros((8 - groups, 128), F32)], axis=0)
    pieces = []
    for _ in range(3):
        pieces.append(rest.astype(BF))
        rest = rest - pieces[-1].astype(F32)
    pieces = jnp.concatenate(pieces, axis=0).astype(F32)
    return pieces, jnp.where((slot >> 7) == iota((8, SLOTS), 0), 1.0, 0.0)


def reply_to(value_all, value_high, slot):
    pieces_all, group = reply_rows(value_all, slot)
    pieces_high, _ = reply_rows(value_high, slot)
    pieces = jnp.concatenate([pieces_all, pieces_high], axis=0).astype(BF)
    pick = (iota((128, SLOTS), 0) == (slot & 127)).astype(BF)
    lines = dot(pieces, pick)
    row = iota((8, SLOTS), 0)
    out = []
    for which in range(2):
        line = lines[which * 24 : which * 24 + 8] + lines[which * 24 + 8 : which * 24 + 16] + lines[which * 24 + 16 : which * 24 + 24]
        found = jnp.sum(line * group, axis=0, keepdims=True)
        out.append(jnp.where(row == 4 * which, found, 0.0))
    return out + [jnp.zeros((8, SLOTS), F32)]


def far_kernel(key_ref, own_ref, other_ref, prev_ref, tail_ref, local_ref, out_ref, by_slot):
    key_cid, key_rank, key_slot = read_meta(key_ref, ROWS)
    cid_col, rank_col = columns(key_cid, key_rank)
    key_all = [jnp.full((HALF, 128), -1.0, F32)] * 2
    key_high = [jnp.full((HALF, 128), -1.0, F32)] * 2
    found = []
    cid, rank, slot = read_meta(tail_ref, HALF)
    work = [(tail_ref, HALF, 1, cid[:, HALF:], rank[:, HALF:], slot - HALF)]
    for ref in (prev_ref, own_ref, other_ref):
        cid, rank, slot = read_meta(ref, ROWS)
        work.append((ref, ROWS, 2, cid, rank, slot))
    for ref, count, halves, cid, rank, slot in work:
        best_all = best_high = None
        for half in range(halves):
            col = slice(half * HALF, (half + 1) * HALF)
            wide_all, wide_high, row_all, row_high = against(key_ref[col, :], cid_col[col], rank_col[col], ref, count, cid, rank)
            key_all[half] = jnp.maximum(key_all[half], wide_all)
            key_high[half] = jnp.maximum(key_high[half], wide_high)
            best_all = row_all if best_all is None else jnp.maximum(best_all, row_all)
            best_high = row_high if best_high is None else jnp.maximum(best_high, row_high)
        found.append((best_all, best_high, slot))
    key_all = jnp.max(jnp.transpose(jnp.concatenate(key_all, axis=0)), axis=0, keepdims=True)
    key_high = jnp.max(jnp.transpose(jnp.concatenate(key_high, axis=0)), axis=0, keepdims=True)
    tail, prev, own, other = found
    own = (jnp.maximum(own[0], local_ref[0:1, :]), jnp.maximum(own[1], local_ref[1:2, :]), own[2])
    rows = []
    for part in (own, other, (key_all, key_high, key_slot), prev, tail):
        rows += reply_to(*part)
    rows.append(jnp.zeros((8, SLOTS), F32))
    by_slot[...] = jnp.transpose(jnp.concatenate(rows, axis=0))
    reply = by_slot[pl.ds(0, DEVICES, stride=8), :]
    for order in range(1, 8):
        reply = reply + pltpu.roll(by_slot[pl.ds(order, DEVICES, stride=8), :], order, 1)
    out_ref[...] = reply + pltpu.roll(by_slot[MAIN:, :], 8, 1)


def answer_kernel(got_ref, route_ref, all_ref, high_ref):
    within = route_ref[5:6, :]
    replies = jnp.transpose(got_ref[...])
    row = iota((24, ROWS), 0)
    best = None
    for role in range(ROLES):
        rest = replies[role * 24 : role * 24 + 24]
        pieces = []
        for _ in range(3):
            pieces.append(rest.astype(BF).astype(F32))
            rest = rest - pieces[-1]
        sender = route_ref[role : role + 1, :]
        lines = dot(jnp.concatenate(pieces, axis=0).astype(BF), (iota((DEVICES, ROWS), 0) == sender).astype(BF))
        lines = jnp.where(sender >= 0, lines[0:24] + lines[24:48] + lines[48:72], -1.0)
        best = lines if best is None else jnp.maximum(best, lines)
    all_ref[...] = jnp.sum(jnp.where(row == within, best, 0.0), axis=0, keepdims=True).reshape(ROWS)
    high_ref[...] = jnp.sum(jnp.where(row == within + 12, best, 0.0), axis=0, keepdims=True).reshape(ROWS)


def call(kernel, out, args, scratch=(), flops=0, name=None, left=(), grant=48):
    moved = sum(a.size * a.dtype.itemsize for a in args)
    many = isinstance(out, list)
    shapes = [jax.ShapeDtypeStruct(*o) for o in (out if many else [out])]
    out_specs = [pl.BlockSpec(memory_space=pltpu.VMEM)] * len(shapes)
    return pl.pallas_call(
        kernel,
        out_shape=shapes if many else shapes[0],
        in_specs=[pl.BlockSpec(memory_space=pl.ANY if i in left else pltpu.VMEM) for i in range(len(args))],
        out_specs=out_specs if many else out_specs[0],
        scratch_shapes=list(scratch),
        compiler_params=pltpu.CompilerParams(vmem_limit_bytes=grant * 1024 * 1024),
        cost_estimate=pl.CostEstimate(flops=flops, bytes_accessed=moved, transcendentals=0),
        name=name,
    )(*args)


def body(embeddings, cluster_id, cluster_rank, dest_slot):
    send, route = call(
        pack_kernel,
        [((MAIN, ROWS + 128), BF), ((8, ROWS), jnp.int32)],
        (embeddings, cluster_id, cluster_rank, dest_slot),
        (
            pltpu.VMEM((ROWS, ROWS), BF),
            pltpu.VMEM((ROWS,), jnp.int32),
            pltpu.VMEM((ROWS,), jnp.int32),
            pltpu.VMEM((ROWS,), jnp.int32),
            pltpu.VMEM((ROWS, ROWS), BF),
            pltpu.VMEM((MAIN, 128), F32),
            pltpu.SemaphoreType.DMA((6,)),
        ),
        name="pack",
        left=(0, 1, 2, 3),
        grant=60,
    )
    got = lax.all_to_all(send, AXES, split_axis=0, concat_axis=0, tiled=True)
    own = call(
        unpack_kernel,
        ((ROWS + META, ROWS), BF),
        (got,),
        (pltpu.VMEM((MAIN, 128), F32), pltpu.VMEM((MAIN, 128), F32)),
        name="unpack",
    )
    everyone = range(DEVICES)
    other = lax.ppermute(own, AXES, routes(lambda t: t ^ 1, everyone))
    key = lax.ppermute(own, AXES, routes(lambda t: t + 2, everyone))
    prev = lax.ppermute(own, AXES, routes(lambda t: t - 1, range(0, DEVICES, 2)))
    tail = lax.ppermute(own[HALF:], AXES, routes(lambda t: t - 2, everyone))
    tile = 2 * ROWS**3
    local = call(local_kernel, ((8, ROWS), F32), (own, other), flops=2 * tile, name="local")
    reply = call(
        far_kernel,
        ((DEVICES, 128), F32),
        (key, own, other, prev, tail, local),
        (pltpu.VMEM((SLOTS, 128), F32),),
        flops=4 * tile,
        name="far",
    )
    answer = lax.all_to_all(reply.reshape(DEVICES, 1, 128), AXES, split_axis=0, concat_axis=0, tiled=True)
    return call(answer_kernel, [((ROWS,), F32)] * 2, (answer.reshape(DEVICES, 128), route), name="answer")


def solution(mesh):
    rows = P(AXES)
    return jax.shard_map(
        body,
        mesh=mesh,
        in_specs=(P(AXES, None), rows, rows, rows),
        out_specs=(rows, rows),
        check_vma=False,
    )
```

time: 105 us -> 98.1 us (0.934)
  local copies, waits for them, and re-layouts: 3.99 us -> 0.04 us
  Pallas kernels: 18.6 us -> 15.3 us
    pallas_call x5, Pallas kernels: 18.6 us -> 15.3 us  [call(): pl.pallas_call(kernel, out_shape=shapes if many else shapes[0], in_specs=...]
    reshape x3 -> x0, local copies, waits for them, and re-layouts: 2.07 us -> none  [body(): a.reshape(1, ROWS)]
    ppermute x1, starting transfers between devices: 1.37 us -> 2.64 us  [body(): lax.ppermute(own, AXES, routes(lambda t: t - 1, range(0, DEVICES, 2)))]
    ppermute x1, starting transfers between devices: 3.73 us -> 2.45 us  [body(): key = lax.ppermute(own, AXES, routes(lambda t: t + 2, everyone))]
    unnamed x2, local copies, waits for them, and re-layouts: 1.27 us -> 0.01 us
  transfers between devices with their start and end apart: 4 -> 4, of which waited for: 1 -> 1; matrix products, arithmetic and copies ran while one was open for 0% -> 0% of each run, Pallas kernels for 2% -> 3%
where the time goes in v1:
time: 98.1 us; the launch traced here: 97.8 us
  blocking collectives  52.4 us (53%)
  waiting for transfers between devices  24 us (24%)
  Pallas kernels  15.3 us (16%)
  starting transfers between devices  5.44 us (6%)
    all_to_all x1, blocking collectives, body(): got = lax.all_to_all(send, AXES, split_axis=0, concat_axis=0, tiled=True)  39 us
    ppermute x1, waiting for transfers between devices, body(): tail = lax.ppermute(own[HALF:], AXES, routes(lambda t: t - 2, everyone))  24 us
    pallas_call x5, Pallas kernels, call(): pl.pallas_call(kernel, out_shape=shapes if many else shapes[0], in_specs=...  15.3 us
    all_to_all x1, blocking collectives, body(): lax.all_to_all(reply.reshape(DEVICES, 1, 128), AXES, split_axis=0, concat...  13.4 us
    ppermute x1, starting transfers between devices, body(): lax.ppermute(own, AXES, routes(lambda t: t - 1, range(0, DEVICES, 2)))  2.64 us
    ppermute x1, starting transfers between devices, body(): key = lax.ppermute(own, AXES, routes(lambda t: t + 2, everyone))  2.45 us
  transfers between devices with their start and end apart: 4, of which 1 were waited for; matrix products, arithmetic and copies ran while one was open for 0% of the time, Pallas kernels for 3%

profile of v1, /device:TPU:1, one launch (start us, length us, event | category | flops | bytes accessed | tf_op | source)
XLA Modules:
  0.0 97.8 jit_solution(16795035142408707361)
XLA Ops:
  0.6 4.5 %pack.1 = (bf16[1024,896]{1,0:T(8,128)(2,1)}, s32[8,768]{1,0:T(8,128)}) custom-call(bf16[768,768]{1,0:T(8,128)(2,1)} %emb_ref.1, s32[768]{0:T(1024)} %cid_ref.1, s32[768]{0:T(1024)} %rank_ref.1, s32[768]{0:T(1024)} %slot_ref.1), custom_call_target="tpu_custom_call" | custom-call | bytes 1188864 | tf_op jit(solution)/shard_map/pack/pallas_call | solution.py:281
  5.1 39.0 %all_to_all.16 = bf16[128,8,896]{2,1,0:T(8,128)(2,1)S(1)} all-to-all(bf16[128,8,896]{2,1,0:T(8,128)(2,1)} %bitcast.9), channel_id=1, replica_groups=mesh['seg'=32,'pair'=4] {'seg','pair'}, dimensions={0} | all-to-all | bytes 3670016 | tf_op jit(solution)/shard_map/all_to_all | solution.py:311
  44.1 2.3 %unpack.1.own_ref = bf16[784,768]{1,0:T(8,128)(2,1)S(1)} custom-call(bf16[1024,896]{1,0:T(8,128)(2,1)S(1)} %bitcast.6), custom_call_target="tpu_custom_call" | custom-call | bytes 1835008 | tf_op jit(solution)/shard_map/unpack/pallas_call | solution.py:281
  46.5 0.1 collective-permute-start.1
  46.6 2.6 %collective-permute-start.2 = (bf16[784,768]{1,0:T(8,128)(2,1)S(1)}, bf16[784,768]{1,0:T(8,128)(2,1)S(1)}, u32[]{:S(2)}, u32[]{:S(2)}) collective-permute-start(bf16[784,768]{1,0:T(8,128)(2,1)S(1)} %unpack.1.own_ref), channel_id=1, source_target_pairs={{83,18},{19,22},{23,38},{39,54},{55,58},{59,120},{121,72},{73,8},{... | collective-permute-start | bytes 3612680 | tf_op jit(solution)/shard_map/ppermute | solution.py:322
  49.2 2.5 %collective-permute-start = (bf16[784,768]{1,0:T(8,128)(2,1)S(1)}, bf16[784,768]{1,0:T(8,128)(2,1)S(1)}, u32[]{:S(2)}, u32[]{:S(2)}) collective-permute-start(bf16[784,768]{1,0:T(8,128)(2,1)S(1)} %unpack.1.own_ref), channel_id=1, source_target_pairs={{22,18},{23,19},{38,22},{39,23},{54,38},{55,39},{58,54},{59,55},{1... | collective-permute-start | bytes 3612680 | tf_op jit(solution)/shard_map/ppermute | solution.py:321
  51.7 0.3 collective-permute-start.3
  52.0 0.0 collective-permute-done.1.other_ref
  52.0 2.5 %local.1.local_ref = f32[8,768]{1,0:T(8,128)S(1)} custom-call(bf16[784,768]{1,0:T(8,128)(2,1)S(1)} %unpack.1.own_ref, bf16[784,768]{1,0:T(8,128)(2,1)S(1)} %collective-permute-done.1.other_ref), custom_call_target="tpu_custom_call" | custom-call | flops 1811939328 | bytes 2408448 | tf_op jit(solution)/shard_map/local/pallas_call | solution.py:281
  54.5 0.0 copy-start
  54.5 24.0 %collective-permute-done.3.tail_ref = bf16[400,768]{1,0:T(8,128)(2,1)S(1)} collective-permute-done((bf16[400,768]{1,0:T(8,128)(2,1)S(1)}, bf16[400,768]{1,0:T(8,128)(2,1)S(1)}, u32[]{:S(2)}, u32[]{:S(2)}) %collective-permute-start.3) | collective-permute-done | bytes 614432 | tf_op jit(solution)/shard_map/ppermute | solution.py:323
  78.5 0.0 collective-permute-done.2.prev_ref
  78.5 0.0 collective-permute-done.key_ref
  78.5 5.0 %far.1 = f32[128,128]{1,0:T(8,128)S(1)} custom-call(bf16[784,768]{1,0:T(8,128)(2,1)S(1)} %collective-permute-done.key_ref, bf16[784,768]{1,0:T(8,128)(2,1)S(1)} %unpack.1.own_ref, bf16[784,768]{1,0:T(8,128)(2,1)S(1)} %collective-permute-done.1.other_ref, bf16[784,768]{1,0:T(8,128)(2,1)S(1)} %collective-permute-done.2.prev_ref, ...), custom_call_target="tpu_custom_call" | custom-call | flops 3623878656 | bytes 5455872 | tf_op jit(solution)/shard_map/far/pallas_call | solution.py:281
  83.5 13.4 %all_to_all.17 = f32[128,1,128]{2,1,0:T(1,128)S(1)} all-to-all(f32[128,1,128]{2,1,0:T(1,128)S(1)} %bitcast.8), channel_id=1, replica_groups=mesh['seg'=32,'pair'=4] {'seg','pair'}, dimensions={0} | all-to-all | bytes 131072 | tf_op jit(solution)/shard_map/all_to_all | solution.py:334
  96.8 0.0 copy-done
  96.8 1.0 %answer.1 = (f32[768]{0:T(1024)}, f32[768]{0:T(1024)}) custom-call(f32[128,128]{1,0:T(8,128)S(1)} %bitcast.7, s32[8,768]{1,0:T(8,128)S(1)} %copy-done), custom_call_target="tpu_custom_call" | custom-call | bytes 90112 | tf_op jit(solution)/shard_map/answer/pallas_call | solution.py:281
  (1 shorter events, 0.0 us)
Async XLA Ops:
  46.5 5.5 %collective-permute-start.1 = (bf16[784,768]{1,0:T(8,128)(2,1)S(1)}, bf16[784,768]{1,0:T(8,128)(2,1)S(1)}, u32[]{:S(2)}, u32[]{:S(2)}) collective-permute-start(bf16[784,768]{1,0:T(8,128)(2,1)S(1)} %unpack.1.own_ref), channel_id=1, source_target_pairs={{19,18},{18,19},{23,22},{22,23},{39,38},{38,39},{55,54},{54,55},{5... | collective-permute-start | bytes 3612680 | tf_op jit(solution)/shard_map/ppermute | solution.py:320
  46.6 32.0 %collective-permute-start.2 = (bf16[784,768]{1,0:T(8,128)(2,1)S(1)}, bf16[784,768]{1,0:T(8,128)(2,1)S(1)}, u32[]{:S(2)}, u32[]{:S(2)}) collective-permute-start(bf16[784,768]{1,0:T(8,128)(2,1)S(1)} %unpack.1.own_ref), channel_id=1, source_target_pairs={{83,18},{19,22},{23,38},{39,54},{55,58},{59,120},{121,72},{73,8},{... | collective-permute-start | bytes 3612680 | tf_op jit(solution)/shard_map/ppermute | solution.py:322
  49.2 29.3 %collective-permute-start = (bf16[784,768]{1,0:T(8,128)(2,1)S(1)}, bf16[784,768]{1,0:T(8,128)(2,1)S(1)}, u32[]{:S(2)}, u32[]{:S(2)}) collective-permute-start(bf16[784,768]{1,0:T(8,128)(2,1)S(1)} %unpack.1.own_ref), channel_id=1, source_target_pairs={{22,18},{23,19},{38,22},{39,23},{54,38},{55,39},{58,54},{59,55},{1... | collective-permute-start | bytes 3612680 | tf_op jit(solution)/shard_map/ppermute | solution.py:321
  51.7 26.8 %collective-permute-start.3 = (bf16[400,768]{1,0:T(8,128)(2,1)S(1)}, bf16[400,768]{1,0:T(8,128)(2,1)S(1)}, u32[]{:S(2)}, u32[]{:S(2)}) collective-permute-start(bf16[400,768]{1,0:T(8,128)(2,1)S(1)} %slice.4), channel_id=1, source_target_pairs={{82,18},{83,19},{18,22},{19,23},{22,38},{23,39},{38,54},{39,55},{5... | collective-permute-start | bytes 1843208 | tf_op jit(solution)/shard_map/ppermute | solution.py:323
  54.5 42.3 %copy-start = (s32[8,768]{1,0:T(8,128)S(1)}, s32[8,768]{1,0:T(8,128)}, u32[]{:S(2)}) copy-start(s32[8,768]{1,0:T(8,128)} %get-tuple-element.5.route_ref) | copy-start | bytes 73732

commit v2 on v1

--- a/solution.py
+++ b/solution.py
@@ -7,15 +7,23 @@
 
 AXES = ("seg", "pair")
 DEVICES = 128
-CHIPS = [
-    (2, 0, 1), (2, 1, 1), (2, 1, 2), (2, 1, 3), (2, 2, 3), (1, 2, 3), (1, 2, 0), (0, 2, 0),
-    (0, 1, 0), (0, 1, 1), (1, 1, 1), (1, 2, 1), (2, 2, 1), (2, 2, 0), (2, 1, 0), (1, 1, 0),
-    (1, 1, 3), (0, 1, 3), (3, 1, 3), (3, 1, 2), (0, 1, 2), (0, 0, 2), (0, 0, 3), (0, 0, 0),
-    (1, 0, 0), (2, 0, 0), (2, 0, 3), (3, 0, 3), (3, 3, 3), (3, 2, 3), (3, 2, 0), (3, 2, 1),
-    (3, 1, 1), (3, 1, 0), (3, 0, 0), (3, 3, 0), (3, 3, 1), (2, 3, 1), (1, 3, 1), (1, 0, 1),
-    (0, 0, 1), (0, 3, 1), (0, 2, 1), (0, 2, 2), (0, 2, 3), (0, 3, 3), (0, 3, 0), (1, 3, 0),
-    (2, 3, 0), (2, 3, 3), (1, 3, 3), (1, 0, 3), (1, 0, 2), (1, 1, 2), (1, 2, 2), (1, 3, 2),
-    (0, 3, 2), (3, 3, 2), (3, 2, 2), (2, 2, 2), (2, 3, 2), (2, 0, 2), (3, 0, 2), (3, 0, 1),
+PLACES = [
+    (3, 3, 3, 0), (2, 3, 3, 0), (3, 3, 0, 0), (2, 3, 0, 0), (3, 0, 0, 0), (2, 0, 0, 0), (3, 0, 1, 0), (2, 0, 1, 0),
+    (3, 0, 2, 0), (2, 0, 2, 0), (3, 0, 3, 0), (2, 0, 3, 0), (3, 1, 3, 0), (2, 1, 3, 0), (3, 1, 0, 0), (2, 1, 0, 0),
+    (3, 1, 1, 0), (2, 1, 1, 0), (3, 1, 2, 0), (2, 1, 2, 0), (3, 2, 2, 0), (2, 2, 2, 0), (3, 2, 3, 0), (2, 2, 3, 0),
+    (3, 2, 0, 0), (2, 2, 0, 0), (3, 2, 1, 0), (2, 2, 1, 0), (3, 3, 1, 0), (2, 3, 1, 0), (3, 3, 2, 0), (2, 3, 2, 0),
+    (2, 3, 2, 1), (1, 3, 2, 1), (2, 2, 2, 1), (1, 2, 2, 1), (2, 2, 1, 1), (1, 2, 1, 1), (2, 1, 1, 1), (1, 1, 1, 1),
+    (2, 0, 1, 1), (1, 0, 1, 1), (2, 3, 1, 1), (1, 3, 1, 1), (2, 3, 0, 1), (1, 3, 0, 1), (2, 2, 0, 1), (1, 2, 0, 1),
+    (2, 1, 0, 1), (1, 1, 0, 1), (2, 0, 0, 1), (1, 0, 0, 1), (2, 0, 3, 1), (1, 0, 3, 1), (2, 3, 3, 1), (1, 3, 3, 1),
+    (2, 2, 3, 1), (1, 2, 3, 1), (2, 1, 3, 1), (1, 1, 3, 1), (2, 1, 2, 1), (1, 1, 2, 1), (2, 0, 2, 1), (1, 0, 2, 1),
+    (1, 0, 2, 0), (0, 0, 2, 0), (1, 0, 1, 0), (0, 0, 1, 0), (1, 0, 0, 0), (0, 0, 0, 0), (1, 3, 0, 0), (0, 3, 0, 0),
+    (1, 3, 3, 0), (0, 3, 3, 0), (1, 3, 2, 0), (0, 3, 2, 0), (1, 3, 1, 0), (0, 3, 1, 0), (1, 2, 1, 0), (0, 2, 1, 0),
+    (1, 2, 0, 0), (0, 2, 0, 0), (1, 2, 3, 0), (0, 2, 3, 0), (1, 2, 2, 0), (0, 2, 2, 0), (1, 1, 2, 0), (0, 1, 2, 0),
+    (1, 1, 1, 0), (0, 1, 1, 0), (1, 1, 0, 0), (0, 1, 0, 0), (1, 1, 3, 0), (0, 1, 3, 0), (1, 0, 3, 0), (0, 0, 3, 0),
+    (0, 0, 3, 1), (3, 0, 3, 1), (0, 0, 0, 1), (3, 0, 0, 1), (0, 1, 0, 1), (3, 1, 0, 1), (0, 2, 0, 1), (3, 2, 0, 1),
+    (0, 3, 0, 1), (3, 3, 0, 1), (0, 3, 1, 1), (3, 3, 1, 1), (0, 0, 1, 1), (3, 0, 1, 1), (0, 1, 1, 1), (3, 1, 1, 1),
+    (0, 2, 1, 1), (3, 2, 1, 1), (0, 2, 2, 1), (3, 2, 2, 1), (0, 3, 2, 1), (3, 3, 2, 1), (0, 0, 2, 1), (3, 0, 2, 1),
+    (0, 1, 2, 1), (3, 1, 2, 1), (0, 1, 3, 1), (3, 1, 3, 1), (0, 2, 3, 1), (3, 2, 3, 1), (0, 3, 3, 1), (3, 3, 3, 1),
 ]
 ROWS = 768
 HALF = 384
@@ -23,26 +31,21 @@
 SLOTS = DEVICES * CAP
 MAIN = DEVICES * 8
 META = 16
-ROLES = 5
+ROLES = 4
 BF = jnp.bfloat16
 F32 = jnp.float32
 NT = (((1,), (1,)), ((), ()))
 
 
-def chip_device(x, y, z):
-    return ((((x & 1) * 4 + z) * 4 + y) << 2) + ((x >> 1) << 1)
-
-
-WALK = [chip_device(*chip) for chip in CHIPS]
+HOLDERS = [((((x & 1) * 4 + z) * 4 + y) << 2) + ((x >> 1) << 1) + core for x, y, z, core in PLACES]
 
 
 def device_of(block):
-    block = block % DEVICES
-    return WALK[block >> 1] + (block & 1)
-
-
-def routes(source_of, targets):
-    return [(device_of(source_of(t)), device_of(t)) for t in targets]
+    return HOLDERS[block % DEVICES]
+
+
+def shift(step):
+    return [(device_of(block + step), device_of(block)) for block in range(DEVICES)]
 
 
 def iota(shape, dim):
@@ -64,12 +67,11 @@
 
 def device_table():
     row, lane = iota((8, DEVICES), 0), iota((8, DEVICES), 1)
-    step = jnp.where(row == 2, -2, jnp.where(row == 3, 1, jnp.where(row == 4, 2, 0)))
-    block = jnp.where(row == 1, lane ^ 1, lane + step) & (DEVICES - 1)
-    chip = block >> 1
-    found = block & 1
-    for index, device in enumerate(WALK):
-        found = found + jnp.where(chip == index, device, 0)
+    step = jnp.where(row == 1, 1, jnp.where(row == 2, -2, jnp.where(row == 3, 2, 0)))
+    block = (lane + step) & (DEVICES - 1)
+    found = jnp.zeros_like(block)
+    for index, device in enumerate(HOLDERS):
+        found = jnp.where(block == index, device, found)
     return found.astype(F32).astype(BF)
 
 
@@ -92,8 +94,8 @@
     within = jnp.sum(to_block.astype(F32) * dot(to_block, earlier), axis=0, keepdims=True).astype(jnp.int32)
     senders = dot(table, to_block).astype(jnp.int32)
     row = iota((8, ROWS), 0)
-    dropped = ((row == 3) & ((block & 1) == 0)) | ((row == 4) & (local < HALF))
-    route_ref[...] = jnp.where(row == 5, within, jnp.where(dropped, -1, senders))
+    dropped = (row == 3) & (local < HALF)
+    route_ref[...] = jnp.where(row == 4, within, jnp.where(dropped, -1, senders))
     device = senders[0:1]
     to_device = (iota((DEVICES, ROWS), 0) == device).astype(BF)
     flat = jnp.where(within < 8, device * 8 + within, -1)
@@ -159,23 +161,47 @@
     return turned[:, 0:1], turned[:, 1:2]
 
 
-def local_kernel(own_ref, other_ref, out_ref):
+def local_kernel(own_ref, out_ref):
     own_cid, own_rank, _ = read_meta(own_ref, ROWS)
+    cid, rank = columns(own_cid, own_rank)
     best_all = jnp.full((8, ROWS), -1.0, F32)
     best_high = jnp.full((8, ROWS), -1.0, F32)
-    for ref in (own_ref, other_ref):
-        cid, rank, _ = read_meta(ref, ROWS)
-        cid, rank = columns(cid, rank)
-        for start in range(0, ROWS, 256):
-            cosine = dot_nt(ref[start : start + 256, :], own_ref[:ROWS, :])
-            c, r = cid[start : start + 256], rank[start : start + 256]
-            near = jnp.where((c == own_cid) & (r != own_rank), cosine, -1.0)
-            high = jnp.where(r < own_rank, near, -1.0)
-            best_all = jnp.maximum(best_all, jnp.max(near.reshape(32, 8, ROWS), axis=0))
-            best_high = jnp.maximum(best_high, jnp.max(high.reshape(32, 8, ROWS), axis=0))
+    for start in range(0, ROWS, HALF):
+        cosine = dot_nt(own_ref[start : start + HALF, :], own_ref[:ROWS, :])
+        c, r = cid[start : start + HALF], rank[start : start + HALF]
+        near = jnp.where((c == own_cid) & (r != own_rank), cosine, -1.0)
+        high = jnp.where(r < own_rank, near, -1.0)
+        best_all = jnp.maximum(best_all, jnp.max(near.reshape(HALF // 8, 8, ROWS), axis=0))
+        best_high = jnp.maximum(best_high, jnp.max(high.reshape(HALF // 8, 8, ROWS), axis=0))
     out_ref[0:1, :] = jnp.max(best_all, axis=0, keepdims=True)
     out_ref[1:2, :] = jnp.max(best_high, axis=0, keepdims=True)
     out_ref[2:, :] = jnp.full((6, ROWS), -1.0, F32)
+
+
+def meet(key_ref, key, others):
+    cid, rank = columns(*key)
+    key_all = [jnp.full((HALF, 128), -1.0, F32)] * 2
+    key_high = [jnp.full((HALF, 128), -1.0, F32)] * 2
+    found = []
+    for ref, count, other_cid, other_rank in others:
+        best = None
+        for half in range(count // HALF):
+            part = slice(half * HALF, (half + 1) * HALF)
+            wide_all, wide_high, row_all, row_high = against(
+                key_ref[part, :], cid[part], rank[part], ref, count, other_cid, other_rank
+            )
+            key_all[half] = jnp.maximum(key_all[half], wide_all)
+            key_high[half] = jnp.maximum(key_high[half], wide_high)
+            best = (row_all, row_high) if best is None else (jnp.maximum(best[0], row_all), jnp.maximum(best[1], row_high))
+        found.append(best)
+    key = tuple(
+        jnp.max(jnp.transpose(jnp.concatenate(wide, axis=0)), axis=0, keepdims=True) for wide in (key_all, key_high)
+    )
+    return key, found
+
+
+def both(left, right):
+    return tuple(jnp.maximum(a, b) for a, b in zip(left, right))
 
 
 def against(key, key_cid, key_rank, other_ref, count, other_cid, other_rank):
@@ -218,35 +244,27 @@
     return out + [jnp.zeros((8, SLOTS), F32)]
 
 
-def far_kernel(key_ref, own_ref, other_ref, prev_ref, tail_ref, local_ref, out_ref, by_slot):
-    key_cid, key_rank, key_slot = read_meta(key_ref, ROWS)
-    cid_col, rank_col = columns(key_cid, key_rank)
-    key_all = [jnp.full((HALF, 128), -1.0, F32)] * 2
-    key_high = [jnp.full((HALF, 128), -1.0, F32)] * 2
-    found = []
-    cid, rank, slot = read_meta(tail_ref, HALF)
-    work = [(tail_ref, HALF, 1, cid[:, HALF:], rank[:, HALF:], slot - HALF)]
-    for ref in (prev_ref, own_ref, other_ref):
-        cid, rank, slot = read_meta(ref, ROWS)
-        work.append((ref, ROWS, 2, cid, rank, slot))
-    for ref, count, halves, cid, rank, slot in work:
-        best_all = best_high = None
-        for half in range(halves):
-            col = slice(half * HALF, (half + 1) * HALF)
-            wide_all, wide_high, row_all, row_high = against(key_ref[col, :], cid_col[col], rank_col[col], ref, count, cid, rank)
-            key_all[half] = jnp.maximum(key_all[half], wide_all)
-            key_high[half] = jnp.maximum(key_high[half], wide_high)
-            best_all = row_all if best_all is None else jnp.maximum(best_all, row_all)
-            best_high = row_high if best_high is None else jnp.maximum(best_high, row_high)
-        found.append((best_all, best_high, slot))
-    key_all = jnp.max(jnp.transpose(jnp.concatenate(key_all, axis=0)), axis=0, keepdims=True)
-    key_high = jnp.max(jnp.transpose(jnp.concatenate(key_high, axis=0)), axis=0, keepdims=True)
-    tail, prev, own, other = found
-    own = (jnp.maximum(own[0], local_ref[0:1, :]), jnp.maximum(own[1], local_ref[1:2, :]), own[2])
+def mate_kernel(own_ref, mate_ref, local_ref, out_ref):
+    own, mate = read_meta(own_ref, ROWS), read_meta(mate_ref, ROWS)
+    mine, (theirs,) = meet(own_ref, own[:2], [(mate_ref, ROWS, *mate[:2])])
+    mine = both(mine, (local_ref[0:1, :], local_ref[1:2, :]))
+    out_ref[...] = jnp.concatenate([*mine, *theirs, jnp.full((4, ROWS), -1.0, F32)], axis=0)
+
+
+def far_kernel(key_ref, own_ref, mate_ref, tail_ref, near_ref, out_ref, by_slot):
+    own, mate, key = (read_meta(ref, ROWS) for ref in (own_ref, mate_ref, key_ref))
+    cid, rank, tail_slot = read_meta(tail_ref, HALF)
+    keys, (tails, mates, owns) = meet(
+        key_ref,
+        key[:2],
+        [(tail_ref, HALF, cid[:, HALF:], rank[:, HALF:]), (mate_ref, ROWS, *mate[:2]), (own_ref, ROWS, *own[:2])],
+    )
+    owns = both(owns, (near_ref[0:1, :], near_ref[1:2, :]))
+    mates = both(mates, (near_ref[2:3, :], near_ref[3:4, :]))
     rows = []
-    for part in (own, other, (key_all, key_high, key_slot), prev, tail):
-        rows += reply_to(*part)
-    rows.append(jnp.zeros((8, SLOTS), F32))
+    for part, slot in ((owns, own[2]), (mates, mate[2]), (keys, key[2]), (tails, tail_slot - HALF)):
+        rows += reply_to(*part, slot)
+    rows.append(jnp.zeros((32, SLOTS), F32))
     by_slot[...] = jnp.transpose(jnp.concatenate(rows, axis=0))
     reply = by_slot[pl.ds(0, DEVICES, stride=8), :]
     for order in range(1, 8):
@@ -255,7 +273,7 @@
 
 
 def answer_kernel(got_ref, route_ref, all_ref, high_ref):
-    within = route_ref[5:6, :]
+    within = route_ref[4:5, :]
     replies = jnp.transpose(got_ref[...])
     row = iota((24, ROWS), 0)
     best = None
@@ -316,19 +334,18 @@
         (pltpu.VMEM((MAIN, 128), F32), pltpu.VMEM((MAIN, 128), F32)),
         name="unpack",
     )
-    everyone = range(DEVICES)
-    other = lax.ppermute(own, AXES, routes(lambda t: t ^ 1, everyone))
-    key = lax.ppermute(own, AXES, routes(lambda t: t + 2, everyone))
-    prev = lax.ppermute(own, AXES, routes(lambda t: t - 1, range(0, DEVICES, 2)))
-    tail = lax.ppermute(own[HALF:], AXES, routes(lambda t: t - 2, everyone))
+    mate = lax.ppermute(own, AXES, shift(-1))
+    key = lax.ppermute(own, AXES, shift(2))
+    tail = lax.ppermute(own[HALF:], AXES, shift(-2))
     tile = 2 * ROWS**3
-    local = call(local_kernel, ((8, ROWS), F32), (own, other), flops=2 * tile, name="local")
+    local = call(local_kernel, ((8, ROWS), F32), (own,), flops=tile, name="local")
+    near = call(mate_kernel, ((8, ROWS), F32), (own, mate, local), flops=tile, name="mate")
     reply = call(
         far_kernel,
         ((DEVICES, 128), F32),
-        (key, own, other, prev, tail, local),
+        (key, own, mate, tail, near),
         (pltpu.VMEM((SLOTS, 128), F32),),
-        flops=4 * tile,
+        flops=3 * tile,
         name="far",
     )
     answer = lax.all_to_all(reply.reshape(DEVICES, 1, 128), AXES, split_axis=0, concat_axis=0, tiled=True)

time: 98.1 us -> 95 us (0.968)
  blocking collectives: 52.4 us -> 57.8 us
  waiting for transfers between devices: 24 us -> 19.5 us
  starting transfers between devices: 5.44 us -> 2.09 us
    all_to_all x1, blocking collectives: 13.4 us -> 18.8 us  [body(): lax.all_to_all(reply.reshape(DEVICES, 1, 128), AXES, split_axis=0, concat...]
    ppermute x4 -> x3, waiting for transfers between devices: 24 us -> 19.5 us  [the longest x1 15.2 us: body(): mate = lax.ppermute(own, AXES, shift(-1))]
    ppermute x4 -> x3, starting transfers between devices: 5.44 us -> 2.09 us  [the longest x1 0.9 us: body(): tail = lax.ppermute(own[HALF:], AXES, shift(-2))]
    pallas_call x5 -> x6, Pallas kernels: 15.3 us -> 14.6 us  [call(): pl.pallas_call(kernel, out_shape=shapes if many else shapes[0], in_specs=...]
  transfers between devices with their start and end apart: 4 -> 3, of which waited for: 1 -> 2; matrix products, arithmetic and copies ran while one was open for 0% -> 0% of each run, Pallas kernels for 3% -> 3%
where the time goes in v2:
time: 95 us; the launch traced here: 94.8 us
  blocking collectives  57.8 us (61%)
  waiting for transfers between devices  19.5 us (21%)
  Pallas kernels  14.6 us (15%)
  starting transfers between devices  2.09 us (2%)
    all_to_all x1, blocking collectives, body(): got = lax.all_to_all(send, AXES, split_axis=0, concat_axis=0, tiled=True)  39 us
    all_to_all x1, blocking collectives, body(): lax.all_to_all(reply.reshape(DEVICES, 1, 128), AXES, split_axis=0, concat...  18.8 us
    ppermute x1, waiting for transfers between devices, body(): mate = lax.ppermute(own, AXES, shift(-1))  15.2 us
    pallas_call x6, Pallas kernels, call(): pl.pallas_call(kernel, out_shape=shapes if many else shapes[0], in_specs=...  14.6 us
    ppermute x1, waiting for transfers between devices, body(): tail = lax.ppermute(own[HALF:], AXES, shift(-2))  4.23 us
  transfers between devices with their start and end apart: 3, of which 2 were waited for; matrix products, arithmetic and copies ran while one was open for 0% of the time, Pallas kernels for 3%

profile of v2, /device:TPU:1, one launch (start us, length us, event | category | flops | bytes accessed | tf_op | source)
XLA Modules:
  0.0 94.8 jit_solution(16221105984584291566)
XLA Ops:
  0.6 4.5 %pack.1 = (bf16[1024,896]{1,0:T(8,128)(2,1)}, s32[8,768]{1,0:T(8,128)}) custom-call(bf16[768,768]{1,0:T(8,128)(2,1)} %emb_ref.1, s32[768]{0:T(1024)} %cid_ref.1, s32[768]{0:T(1024)} %rank_ref.1, s32[768]{0:T(1024)} %slot_ref.1), custom_call_target="tpu_custom_call" | custom-call | bytes 1188864 | tf_op jit(solution)/shard_map/pack/pallas_call | solution.py:299
  5.1 39.0 %all_to_all.16 = bf16[128,8,896]{2,1,0:T(8,128)(2,1)S(1)} all-to-all(bf16[128,8,896]{2,1,0:T(8,128)(2,1)} %bitcast.9), channel_id=1, replica_groups=mesh['seg'=32,'pair'=4] {'seg','pair'}, dimensions={0} | all-to-all | bytes 3670016 | tf_op jit(solution)/shard_map/all_to_all | solution.py:329
  44.1 2.3 %unpack.1.own_ref = bf16[784,768]{1,0:T(8,128)(2,1)S(1)} custom-call(bf16[1024,896]{1,0:T(8,128)(2,1)S(1)} %bitcast.6), custom_call_target="tpu_custom_call" | custom-call | bytes 1835008 | tf_op jit(solution)/shard_map/unpack/pallas_call | solution.py:299
  46.5 0.4 collective-permute-start.1
  46.8 0.8 collective-permute-start
  47.7 0.9 collective-permute-start.2
  48.6 1.4 %local.1.local_ref = f32[8,768]{1,0:T(8,128)S(1)} custom-call(bf16[784,768]{1,0:T(8,128)(2,1)S(1)} %unpack.1.own_ref), custom_call_target="tpu_custom_call" | custom-call | flops 905969664 | bytes 1204224 | tf_op jit(solution)/shard_map/local/pallas_call | solution.py:299
  50.0 15.2 %collective-permute-done.1.mate_ref = bf16[784,768]{1,0:T(8,128)(2,1)S(1)} collective-permute-done((bf16[784,768]{1,0:T(8,128)(2,1)S(1)}, bf16[784,768]{1,0:T(8,128)(2,1)S(1)}, u32[]{:S(2)}, u32[]{:S(2)}) %collective-permute-start.1) | collective-permute-done | bytes 1204256 | tf_op jit(solution)/shard_map/ppermute | solution.py:337
  65.3 1.5 %mate.1.near_ref = f32[8,768]{1,0:T(8,128)S(1)} custom-call(bf16[784,768]{1,0:T(8,128)(2,1)S(1)} %unpack.1.own_ref, bf16[784,768]{1,0:T(8,128)(2,1)S(1)} %collective-permute-done.1.mate_ref, f32[8,768]{1,0:T(8,128)S(1)} %local.1.local_ref), custom_call_target="tpu_custom_call" | custom-call | flops 905969664 | bytes 2433024 | tf_op jit(solution)/shard_map/mate/pallas_call | solution.py:299
  66.8 0.0 copy-start
  66.8 4.2 %collective-permute-done.2.tail_ref = bf16[400,768]{1,0:T(8,128)(2,1)S(1)} collective-permute-done((bf16[400,768]{1,0:T(8,128)(2,1)S(1)}, bf16[400,768]{1,0:T(8,128)(2,1)S(1)}, u32[]{:S(2)}, u32[]{:S(2)}) %collective-permute-start.2) | collective-permute-done | bytes 614432 | tf_op jit(solution)/shard_map/ppermute | solution.py:339
  71.1 0.0 collective-permute-done.key_ref
  71.1 3.9 %far.1 = f32[128,128]{1,0:T(8,128)S(1)} custom-call(bf16[784,768]{1,0:T(8,128)(2,1)S(1)} %collective-permute-done.key_ref, bf16[784,768]{1,0:T(8,128)(2,1)S(1)} %unpack.1.own_ref, bf16[784,768]{1,0:T(8,128)(2,1)S(1)} %collective-permute-done.1.mate_ref, bf16[400,768]{1,0:T(8,128)(2,1)S(1)} %collective-permute-done.2.tail_ref, f32[8,768]{1,0:T(8,128)S(1)} %mate.1.near_ref), custom_call_target="tpu_custom_call" | custom-call | flops 2717908992 | bytes 4251648 | tf_op jit(solution)/shard_map/far/pallas_call | solution.py:299
  75.0 18.8 %all_to_all.17 = f32[128,1,128]{2,1,0:T(1,128)S(1)} all-to-all(f32[128,1,128]{2,1,0:T(1,128)S(1)} %bitcast.8), channel_id=1, replica_groups=mesh['seg'=32,'pair'=4] {'seg','pair'}, dimensions={0} | all-to-all | bytes 131072 | tf_op jit(solution)/shard_map/all_to_all | solution.py:351
  93.8 0.0 copy-done
  93.8 0.9 answer.1
  (1 shorter events, 0.0 us)
Async XLA Ops:
  46.5 18.8 %collective-permute-start.1 = (bf16[784,768]{1,0:T(8,128)(2,1)S(1)}, bf16[784,768]{1,0:T(8,128)(2,1)S(1)}, u32[]{:S(2)}, u32[]{:S(2)}) collective-permute-start(bf16[784,768]{1,0:T(8,128)(2,1)S(1)} %unpack.1.own_ref), channel_id=1, source_target_pairs={{127,126},{126,62},{62,78},{78,14},{14,66},{66,2},{2,82},{82,18},{... | collective-permute-start | bytes 3612680 | tf_op jit(solution)/shard_map/ppermute | solution.py:337
  46.8 24.2 %collective-permute-start = (bf16[784,768]{1,0:T(8,128)(2,1)S(1)}, bf16[784,768]{1,0:T(8,128)(2,1)S(1)}, u32[]{:S(2)}, u32[]{:S(2)}) collective-permute-start(bf16[784,768]{1,0:T(8,128)(2,1)S(1)} %unpack.1.own_ref), channel_id=1, source_target_pairs={{78,126},{14,62},{66,78},{2,14},{82,66},{18,2},{98,82},{34,18},{11... | collective-permute-start | bytes 3612680 | tf_op jit(solution)/shard_map/ppermute | solution.py:338
  47.7 23.4 %collective-permute-start.2 = (bf16[400,768]{1,0:T(8,128)(2,1)S(1)}, bf16[400,768]{1,0:T(8,128)(2,1)S(1)}, u32[]{:S(2)}, u32[]{:S(2)}) collective-permute-start(bf16[400,768]{1,0:T(8,128)(2,1)S(1)} %slice.4), channel_id=1, source_target_pairs={{61,126},{127,62},{126,78},{62,14},{78,66},{14,2},{66,82},{2,18},{... | collective-permute-start | bytes 1843208 | tf_op jit(solution)/shard_map/ppermute | solution.py:339
  66.8 27.0 %copy-start = (s32[8,768]{1,0:T(8,128)S(1)}, s32[8,768]{1,0:T(8,128)}, u32[]{:S(2)}) copy-start(s32[8,768]{1,0:T(8,128)} %get-tuple-element.5.route_ref) | copy-start | bytes 73732

commit v3 on v2

--- a/solution.py
+++ b/solution.py
@@ -8,22 +8,22 @@
 AXES = ("seg", "pair")
 DEVICES = 128
 PLACES = [
-    (3, 3, 3, 0), (2, 3, 3, 0), (3, 3, 0, 0), (2, 3, 0, 0), (3, 0, 0, 0), (2, 0, 0, 0), (3, 0, 1, 0), (2, 0, 1, 0),
-    (3, 0, 2, 0), (2, 0, 2, 0), (3, 0, 3, 0), (2, 0, 3, 0), (3, 1, 3, 0), (2, 1, 3, 0), (3, 1, 0, 0), (2, 1, 0, 0),
-    (3, 1, 1, 0), (2, 1, 1, 0), (3, 1, 2, 0), (2, 1, 2, 0), (3, 2, 2, 0), (2, 2, 2, 0), (3, 2, 3, 0), (2, 2, 3, 0),
-    (3, 2, 0, 0), (2, 2, 0, 0), (3, 2, 1, 0), (2, 2, 1, 0), (3, 3, 1, 0), (2, 3, 1, 0), (3, 3, 2, 0), (2, 3, 2, 0),
-    (2, 3, 2, 1), (1, 3, 2, 1), (2, 2, 2, 1), (1, 2, 2, 1), (2, 2, 1, 1), (1, 2, 1, 1), (2, 1, 1, 1), (1, 1, 1, 1),
-    (2, 0, 1, 1), (1, 0, 1, 1), (2, 3, 1, 1), (1, 3, 1, 1), (2, 3, 0, 1), (1, 3, 0, 1), (2, 2, 0, 1), (1, 2, 0, 1),
-    (2, 1, 0, 1), (1, 1, 0, 1), (2, 0, 0, 1), (1, 0, 0, 1), (2, 0, 3, 1), (1, 0, 3, 1), (2, 3, 3, 1), (1, 3, 3, 1),
-    (2, 2, 3, 1), (1, 2, 3, 1), (2, 1, 3, 1), (1, 1, 3, 1), (2, 1, 2, 1), (1, 1, 2, 1), (2, 0, 2, 1), (1, 0, 2, 1),
-    (1, 0, 2, 0), (0, 0, 2, 0), (1, 0, 1, 0), (0, 0, 1, 0), (1, 0, 0, 0), (0, 0, 0, 0), (1, 3, 0, 0), (0, 3, 0, 0),
-    (1, 3, 3, 0), (0, 3, 3, 0), (1, 3, 2, 0), (0, 3, 2, 0), (1, 3, 1, 0), (0, 3, 1, 0), (1, 2, 1, 0), (0, 2, 1, 0),
-    (1, 2, 0, 0), (0, 2, 0, 0), (1, 2, 3, 0), (0, 2, 3, 0), (1, 2, 2, 0), (0, 2, 2, 0), (1, 1, 2, 0), (0, 1, 2, 0),
-    (1, 1, 1, 0), (0, 1, 1, 0), (1, 1, 0, 0), (0, 1, 0, 0), (1, 1, 3, 0), (0, 1, 3, 0), (1, 0, 3, 0), (0, 0, 3, 0),
-    (0, 0, 3, 1), (3, 0, 3, 1), (0, 0, 0, 1), (3, 0, 0, 1), (0, 1, 0, 1), (3, 1, 0, 1), (0, 2, 0, 1), (3, 2, 0, 1),
-    (0, 3, 0, 1), (3, 3, 0, 1), (0, 3, 1, 1), (3, 3, 1, 1), (0, 0, 1, 1), (3, 0, 1, 1), (0, 1, 1, 1), (3, 1, 1, 1),
-    (0, 2, 1, 1), (3, 2, 1, 1), (0, 2, 2, 1), (3, 2, 2, 1), (0, 3, 2, 1), (3, 3, 2, 1), (0, 0, 2, 1), (3, 0, 2, 1),
-    (0, 1, 2, 1), (3, 1, 2, 1), (0, 1, 3, 1), (3, 1, 3, 1), (0, 2, 3, 1), (3, 2, 3, 1), (0, 3, 3, 1), (3, 3, 3, 1),
+    (3, 0, 1, 1), (0, 0, 1, 1), (3, 1, 1, 1), (0, 1, 1, 1), (3, 2, 1, 1), (0, 2, 1, 1), (3, 2, 2, 1), (0, 2, 2, 1),
+    (3, 3, 2, 1), (0, 3, 2, 1), (3, 0, 2, 1), (0, 0, 2, 1), (3, 1, 2, 1), (0, 1, 2, 1), (3, 1, 3, 1), (0, 1, 3, 1),
+    (3, 2, 3, 1), (0, 2, 3, 1), (3, 3, 3, 1), (0, 3, 3, 1), (3, 0, 3, 1), (0, 0, 3, 1), (3, 0, 0, 1), (0, 0, 0, 1),
+    (3, 1, 0, 1), (0, 1, 0, 1), (3, 2, 0, 1), (0, 2, 0, 1), (3, 3, 0, 1), (0, 3, 0, 1), (3, 3, 1, 1), (0, 3, 1, 1),
+    (0, 3, 1, 0), (1, 3, 1, 0), (0, 2, 1, 0), (1, 2, 1, 0), (0, 2, 0, 0), (1, 2, 0, 0), (0, 2, 3, 0), (1, 2, 3, 0),
+    (0, 2, 2, 0), (1, 2, 2, 0), (0, 1, 2, 0), (1, 1, 2, 0), (0, 1, 1, 0), (1, 1, 1, 0), (0, 1, 0, 0), (1, 1, 0, 0),
+    (0, 1, 3, 0), (1, 1, 3, 0), (0, 0, 3, 0), (1, 0, 3, 0), (0, 0, 2, 0), (1, 0, 2, 0), (0, 0, 1, 0), (1, 0, 1, 0),
+    (0, 0, 0, 0), (1, 0, 0, 0), (0, 3, 0, 0), (1, 3, 0, 0), (0, 3, 3, 0), (1, 3, 3, 0), (0, 3, 2, 0), (1, 3, 2, 0),
+    (1, 3, 2, 1), (2, 3, 2, 1), (1, 2, 2, 1), (2, 2, 2, 1), (1, 2, 1, 1), (2, 2, 1, 1), (1, 1, 1, 1), (2, 1, 1, 1),
+    (1, 0, 1, 1), (2, 0, 1, 1), (1, 3, 1, 1), (2, 3, 1, 1), (1, 3, 0, 1), (2, 3, 0, 1), (1, 2, 0, 1), (2, 2, 0, 1),
+    (1, 1, 0, 1), (2, 1, 0, 1), (1, 0, 0, 1), (2, 0, 0, 1), (1, 0, 3, 1), (2, 0, 3, 1), (1, 3, 3, 1), (2, 3, 3, 1),
+    (1, 2, 3, 1), (2, 2, 3, 1), (1, 1, 3, 1), (2, 1, 3, 1), (1, 1, 2, 1), (2, 1, 2, 1), (1, 0, 2, 1), (2, 0, 2, 1),
+    (2, 0, 2, 0), (3, 0, 2, 0), (2, 0, 3, 0), (3, 0, 3, 0), (2, 1, 3, 0), (3, 1, 3, 0), (2, 1, 0, 0), (3, 1, 0, 0),
+    (2, 1, 1, 0), (3, 1, 1, 0), (2, 1, 2, 0), (3, 1, 2, 0), (2, 2, 2, 0), (3, 2, 2, 0), (2, 2, 3, 0), (3, 2, 3, 0),
+    (2, 2, 0, 0), (3, 2, 0, 0), (2, 2, 1, 0), (3, 2, 1, 0), (2, 3, 1, 0), (3, 3, 1, 0), (2, 3, 2, 0), (3, 3, 2, 0),
+    (2, 3, 3, 0), (3, 3, 3, 0), (2, 3, 0, 0), (3, 3, 0, 0), (2, 0, 0, 0), (3, 0, 0, 0), (2, 0, 1, 0), (3, 0, 1, 0),
 ]
 ROWS = 768
 HALF = 384
@@ -120,7 +120,7 @@
     out_ref[:, ROWS:] = extra[...].astype(BF)
 
 
-def unpack_kernel(got_ref, out_ref, extra, spread):
+def unpack_kernel(got_ref, out_ref, first_ref, extra, spread):
     extra[...] = got_ref[:, ROWS:].astype(F32)
     ninth_rows = jnp.concatenate([extra[pl.ds(part, DEVICES, stride=8), :] for part in range(6)], axis=1).astype(BF)
     meta = extra[pl.ds(6, DEVICES, stride=8), :]
@@ -144,6 +144,8 @@
     out_ref[ROWS + 9 : ROWS + 10, :] = cols[1:2, :ROWS]
     out_ref[ROWS + 10 : ROWS + 11, :HALF] = cols[0:1, ROWS:]
     out_ref[ROWS + 11 : ROWS + 12, :HALF] = cols[1:2, ROWS:]
+    first_ref[:HALF, :] = out_ref[:HALF, :]
+    first_ref[HALF:, :] = out_ref[ROWS:, :]
 
 
 def read_meta(block_ref, rows):
@@ -156,7 +158,7 @@
 
 
 def columns(cid, rank):
-    both = jnp.concatenate([cid, rank, jnp.zeros((6, ROWS), F32)], axis=0)
+    both = jnp.concatenate([cid, rank, jnp.zeros((6, cid.shape[1]), F32)], axis=0)
     turned = jnp.transpose(both)
     return turned[:, 0:1], turned[:, 1:2]
 
@@ -178,26 +180,20 @@
     out_ref[2:, :] = jnp.full((6, ROWS), -1.0, F32)
 
 
-def meet(key_ref, key, others):
-    cid, rank = columns(*key)
-    key_all = [jnp.full((HALF, 128), -1.0, F32)] * 2
-    key_high = [jnp.full((HALF, 128), -1.0, F32)] * 2
-    found = []
+def meet(key, ids, others):
+    cid, rank = columns(*ids)
+    key_all = jnp.full((HALF, 128), -1.0, F32)
+    key_high, found = key_all, []
     for ref, count, other_cid, other_rank in others:
-        best = None
-        for half in range(count // HALF):
-            part = slice(half * HALF, (half + 1) * HALF)
-            wide_all, wide_high, row_all, row_high = against(
-                key_ref[part, :], cid[part], rank[part], ref, count, other_cid, other_rank
-            )
-            key_all[half] = jnp.maximum(key_all[half], wide_all)
-            key_high[half] = jnp.maximum(key_high[half], wide_high)
-            best = (row_all, row_high) if best is None else (jnp.maximum(best[0], row_all), jnp.maximum(best[1], row_high))
-        found.append(best)
-    key = tuple(
-        jnp.max(jnp.transpose(jnp.concatenate(wide, axis=0)), axis=0, keepdims=True) for wide in (key_all, key_high)
-    )
-    return key, found
+        wide_all, wide_high, row_all, row_high = against(key, cid, rank, ref, count, other_cid, other_rank)
+        key_all, key_high = jnp.maximum(key_all, wide_all), jnp.maximum(key_high, wide_high)
+        found.append((row_all, row_high))
+    return tuple(jnp.max(jnp.transpose(wide), axis=0, keepdims=True) for wide in (key_all, key_high)), found
+
+
+def half_ids(ids, half):
+    part = slice(half * HALF, (half + 1) * HALF)
+    return ids[0][:, part], ids[1][:, part]
 
 
 def both(left, right):
@@ -246,23 +242,43 @@
 
 def mate_kernel(own_ref, mate_ref, local_ref, out_ref):
     own, mate = read_meta(own_ref, ROWS), read_meta(mate_ref, ROWS)
-    mine, (theirs,) = meet(own_ref, own[:2], [(mate_ref, ROWS, *mate[:2])])
+    mine, theirs = [], None
+    for half in range(2):
+        rows = own_ref[half * HALF : (half + 1) * HALF, :]
+        keys, (found,) = meet(rows, half_ids(own, half), [(mate_ref, ROWS, *mate[:2])])
+        mine.append(keys)
+        theirs = found if theirs is None else both(theirs, found)
+    mine = [jnp.concatenate([mine[0][i], mine[1][i]], axis=1) for i in range(2)]
     mine = both(mine, (local_ref[0:1, :], local_ref[1:2, :]))
     out_ref[...] = jnp.concatenate([*mine, *theirs, jnp.full((4, ROWS), -1.0, F32)], axis=0)
 
 
-def far_kernel(key_ref, own_ref, mate_ref, tail_ref, near_ref, out_ref, by_slot):
-    own, mate, key = (read_meta(ref, ROWS) for ref in (own_ref, mate_ref, key_ref))
-    cid, rank, tail_slot = read_meta(tail_ref, HALF)
+def far_first_kernel(key_ref, own_ref, mate_ref, tail_ref, near_ref, out_ref):
+    own, mate = read_meta(own_ref, ROWS), read_meta(mate_ref, ROWS)
+    key, tail = read_meta(key_ref, HALF), read_meta(tail_ref, HALF)
     keys, (tails, mates, owns) = meet(
-        key_ref,
-        key[:2],
-        [(tail_ref, HALF, cid[:, HALF:], rank[:, HALF:]), (mate_ref, ROWS, *mate[:2]), (own_ref, ROWS, *own[:2])],
+        key_ref[:HALF, :],
+        half_ids(key, 0),
+        [(tail_ref, HALF, *half_ids(tail, 1)), (mate_ref, ROWS, *mate[:2]), (own_ref, ROWS, *own[:2])],
     )
     owns = both(owns, (near_ref[0:1, :], near_ref[1:2, :]))
     mates = both(mates, (near_ref[2:3, :], near_ref[3:4, :]))
+    ends = [jnp.concatenate([keys[i], tails[i]], axis=1) for i in range(2)]
+    out_ref[...] = jnp.concatenate([*owns, *mates, *ends, jnp.zeros((2, ROWS), F32)], axis=0)
+
+
+def far_second_kernel(key_ref, own_ref, mate_ref, tail_ref, first_ref, out_ref, by_slot):
+    own, mate = read_meta(own_ref, ROWS), read_meta(mate_ref, ROWS)
+    key, tail = read_meta(key_ref, HALF), read_meta(tail_ref, HALF)
+    keys, (mates, owns) = meet(
+        key_ref[:HALF, :], half_ids(key, 1), [(mate_ref, ROWS, *mate[:2]), (own_ref, ROWS, *own[:2])]
+    )
+    line = [first_ref[i : i + 1, :] for i in range(6)]
+    owns, mates = both(owns, line[0:2]), both(mates, line[2:4])
+    keys = [jnp.concatenate([line[4 + i][:, :HALF], keys[i]], axis=1) for i in range(2)]
+    tails = [line[4 + i][:, HALF:] for i in range(2)]
     rows = []
-    for part, slot in ((owns, own[2]), (mates, mate[2]), (keys, key[2]), (tails, tail_slot - HALF)):
+    for part, slot in ((owns, own[2]), (mates, mate[2]), (keys, key[2]), (tails, tail[2] - HALF)):
         rows += reply_to(*part, slot)
     rows.append(jnp.zeros((32, SLOTS), F32))
     by_slot[...] = jnp.transpose(jnp.concatenate(rows, axis=0))
@@ -327,26 +343,29 @@
         grant=60,
     )
     got = lax.all_to_all(send, AXES, split_axis=0, concat_axis=0, tiled=True)
-    own = call(
+    own, first = call(
         unpack_kernel,
-        ((ROWS + META, ROWS), BF),
+        [((ROWS + META, ROWS), BF), ((HALF + META, ROWS), BF)],
         (got,),
         (pltpu.VMEM((MAIN, 128), F32), pltpu.VMEM((MAIN, 128), F32)),
         name="unpack",
     )
+    second = own[HALF:]
     mate = lax.ppermute(own, AXES, shift(-1))
-    key = lax.ppermute(own, AXES, shift(2))
-    tail = lax.ppermute(own[HALF:], AXES, shift(-2))
+    key1 = lax.ppermute(first, AXES, shift(2))
+    tail = lax.ppermute(second, AXES, shift(-2))
+    key2 = lax.ppermute(second, AXES, shift(2))
     tile = 2 * ROWS**3
     local = call(local_kernel, ((8, ROWS), F32), (own,), flops=tile, name="local")
     near = call(mate_kernel, ((8, ROWS), F32), (own, mate, local), flops=tile, name="mate")
+    lines = call(far_first_kernel, ((8, ROWS), F32), (key1, own, mate, tail, near), flops=tile, name="far_first")
     reply = call(
-        far_kernel,
+        far_second_kernel,
         ((DEVICES, 128), F32),
-        (key, own, mate, tail, near),
+        (key2, own, mate, tail, lines),
         (pltpu.VMEM((SLOTS, 128), F32),),
-        flops=3 * tile,
-        name="far",
+        flops=tile,
+        name="far_second",
     )
     answer = lax.all_to_all(reply.reshape(DEVICES, 1, 128), AXES, split_axis=0, concat_axis=0, tiled=True)
     return call(answer_kernel, [((ROWS,), F32)] * 2, (answer.reshape(DEVICES, 128), route), name="answer")

time: 95 us -> 92.2 us (0.971)
  waiting for transfers between devices: 19.5 us -> 9.92 us
  starting transfers between devices: 2.09 us -> 5.51 us
  blocking collectives: 57.8 us -> 61 us
    ppermute x1, waiting for transfers between devices: 15.2 us -> 9.91 us  [body(): mate = lax.ppermute(own, AXES, shift(-1))]
    ppermute x2 -> x3, waiting for transfers between devices: 4.23 us -> 0.01 us  [the longest x1 0.01 us: body(): tail = lax.ppermute(second, AXES, shift(-2))]
    ppermute x2 -> x3, starting transfers between devices: 1.72 us -> 5.25 us  [the longest x1 2.5 us: body(): key2 = lax.ppermute(second, AXES, shift(2))]
    all_to_all x1, blocking collectives: 18.8 us -> 22 us  [body(): lax.all_to_all(reply.reshape(DEVICES, 1, 128), AXES, split_axis=0, concat...]
    pallas_call x6 -> x7, Pallas kernels: 14.6 us -> 14.8 us  [call(): pl.pallas_call(kernel, out_shape=shapes if many else shapes[0], in_specs=...]
  transfers between devices with their start and end apart: 3 -> 4, of which waited for: 2 -> 1; matrix products, arithmetic and copies ran while one was open for 0% -> 0% of each run, Pallas kernels for 3% -> 5%
where the time goes in v3:
time: 92.2 us; the launch traced here: 92 us
  blocking collectives  61 us (66%)
  Pallas kernels  14.8 us (16%)
  waiting for transfers between devices  9.92 us (11%)
  starting transfers between devices  5.51 us (6%)
    all_to_all x1, blocking collectives, body(): got = lax.all_to_all(send, AXES, split_axis=0, concat_axis=0, tiled=True)  39 us
    all_to_all x1, blocking collectives, body(): lax.all_to_all(reply.reshape(DEVICES, 1, 128), AXES, split_axis=0, concat...  22 us
    pallas_call x7, Pallas kernels, call(): pl.pallas_call(kernel, out_shape=shapes if many else shapes[0], in_specs=...  14.8 us
    ppermute x1, waiting for transfers between devices, body(): mate = lax.ppermute(own, AXES, shift(-1))  9.91 us
    ppermute x1, starting transfers between devices, body(): key2 = lax.ppermute(second, AXES, shift(2))  2.5 us
  transfers between devices with their start and end apart: 4, of which 1 were waited for; matrix products, arithmetic and copies ran while one was open for 0% of the time, Pallas kernels for 5%

profile of v3, /device:TPU:1, one launch (start us, length us, event | category | flops | bytes accessed | tf_op | source)
XLA Modules:
  0.0 92.0 jit_solution(14673754235146627515)
XLA Ops:
  0.6 4.5 %pack.1 = (bf16[1024,896]{1,0:T(8,128)(2,1)}, s32[8,768]{1,0:T(8,128)}) custom-call(bf16[768,768]{1,0:T(8,128)(2,1)} %emb_ref.1, s32[768]{0:T(1024)} %cid_ref.1, s32[768]{0:T(1024)} %rank_ref.1, s32[768]{0:T(1024)} %slot_ref.1), custom_call_target="tpu_custom_call" | custom-call | bytes 1188864 | tf_op jit(solution)/shard_map/pack/pallas_call | solution.py:315
  5.1 39.0 %all_to_all.16 = bf16[128,8,896]{2,1,0:T(8,128)(2,1)S(1)} all-to-all(bf16[128,8,896]{2,1,0:T(8,128)(2,1)} %bitcast.9), channel_id=1, replica_groups=mesh['seg'=32,'pair'=4] {'seg','pair'}, dimensions={0} | all-to-all | bytes 3670016 | tf_op jit(solution)/shard_map/all_to_all | solution.py:345
  44.1 2.3 %unpack.1 = (bf16[784,768]{1,0:T(8,128)(2,1)S(1)}, bf16[400,768]{1,0:T(8,128)(2,1)S(1)}) custom-call(bf16[1024,896]{1,0:T(8,128)(2,1)S(1)} %bitcast.6), custom_call_target="tpu_custom_call" | custom-call | bytes 1835008 | tf_op jit(solution)/shard_map/unpack/pallas_call | solution.py:315
  46.5 0.3 collective-permute-start.1
  46.8 1.3 %collective-permute-start.2 = (bf16[400,768]{1,0:T(8,128)(2,1)S(1)}, bf16[400,768]{1,0:T(8,128)(2,1)S(1)}, u32[]{:S(2)}, u32[]{:S(2)}) collective-permute-start(bf16[400,768]{1,0:T(8,128)(2,1)S(1)} %slice.3), channel_id=1, source_target_pairs={{18,83},{82,17},{83,87},{17,21},{87,91},{21,25},{91,107},{25,41},{... | collective-permute-start | bytes 1843208 | tf_op jit(solution)/shard_map/ppermute | solution.py:356
  48.1 1.4 %collective-permute-start.3 = (bf16[400,768]{1,0:T(8,128)(2,1)S(1)}, bf16[400,768]{1,0:T(8,128)(2,1)S(1)}, u32[]{:S(2)}, u32[]{:S(2)}) collective-permute-start(bf16[400,768]{1,0:T(8,128)(2,1)S(1)} %get-tuple-element.8), channel_id=1, source_target_pairs={{87,83},{21,17},{91,87},{25,21},{107,91},{41,25},{111,107},{45,41}... | collective-permute-start | bytes 1843208 | tf_op jit(solution)/shard_map/ppermute | solution.py:355
  49.5 2.5 %collective-permute-start = (bf16[400,768]{1,0:T(8,128)(2,1)S(1)}, bf16[400,768]{1,0:T(8,128)(2,1)S(1)}, u32[]{:S(2)}, u32[]{:S(2)}) collective-permute-start(bf16[400,768]{1,0:T(8,128)(2,1)S(1)} %slice.3), channel_id=1, source_target_pairs={{87,83},{21,17},{91,87},{25,21},{107,91},{41,25},{111,107},{45,41}... | collective-permute-start | bytes 1843208 | tf_op jit(solution)/shard_map/ppermute | solution.py:357
  52.0 1.4 %local.1.local_ref = f32[8,768]{1,0:T(8,128)S(1)} custom-call(bf16[784,768]{1,0:T(8,128)(2,1)S(1)} %get-tuple-element.7.own_ref), custom_call_target="tpu_custom_call" | custom-call | flops 905969664 | bytes 1204224 | tf_op jit(solution)/shard_map/local/pallas_call | solution.py:315
  53.4 9.9 %collective-permute-done.1.mate_ref = bf16[784,768]{1,0:T(8,128)(2,1)S(1)} collective-permute-done((bf16[784,768]{1,0:T(8,128)(2,1)S(1)}, bf16[784,768]{1,0:T(8,128)(2,1)S(1)}, u32[]{:S(2)}, u32[]{:S(2)}) %collective-permute-start.1) | collective-permute-done | bytes 1204256 | tf_op jit(solution)/shard_map/ppermute | solution.py:354
  63.4 1.5 %mate.1.near_ref = f32[8,768]{1,0:T(8,128)S(1)} custom-call(bf16[784,768]{1,0:T(8,128)(2,1)S(1)} %get-tuple-element.7.own_ref, bf16[784,768]{1,0:T(8,128)(2,1)S(1)} %collective-permute-done.1.mate_ref, f32[8,768]{1,0:T(8,128)S(1)} %local.1.local_ref), custom_call_target="tpu_custom_call" | custom-call | flops 905969664 | bytes 2433024 | tf_op jit(solution)/shard_map/mate/pallas_call | solution.py:315
  64.9 0.0 collective-permute-done.2.tail_ref
  64.9 0.0 collective-permute-done.3.key_ref
  64.9 1.9 %far_first.1.first_ref = f32[8,768]{1,0:T(8,128)S(1)} custom-call(bf16[400,768]{1,0:T(8,128)(2,1)S(1)} %collective-permute-done.3.key_ref, bf16[784,768]{1,0:T(8,128)(2,1)S(1)} %get-tuple-element.7.own_ref, bf16[784,768]{1,0:T(8,128)(2,1)S(1)} %collective-permute-done.1.mate_ref, bf16[400,768]{1,0:T(8,128)(2,1)S(1)} %collective-permute-done.2.tail_ref, ...), custom_call_target="tpu_custom_call" | custom-call | flops 905969664 | bytes 3661824 | tf_op jit(solution)/shard_map/far_first/pallas_call | solution.py:315
  66.7 0.0 copy-start
  66.8 0.0 collective-permute-done.key_ref
  66.8 2.3 %far_second.1 = f32[128,128]{1,0:T(8,128)S(1)} custom-call(bf16[400,768]{1,0:T(8,128)(2,1)S(1)} %collective-permute-done.key_ref, bf16[784,768]{1,0:T(8,128)(2,1)S(1)} %get-tuple-element.7.own_ref, bf16[784,768]{1,0:T(8,128)(2,1)S(1)} %collective-permute-done.1.mate_ref, bf16[400,768]{1,0:T(8,128)(2,1)S(1)} %collective-permute-done.2.tail_ref, ...), custom_call_target="tpu_custom_call" | custom-call | flops 905969664 | bytes 3661824 | tf_op jit(solution)/shard_map/far_second/pallas_call | solution.py:315
  69.0 22.0 %all_to_all.17 = f32[128,1,128]{2,1,0:T(1,128)S(1)} all-to-all(f32[128,1,128]{2,1,0:T(1,128)S(1)} %bitcast.7), channel_id=1, replica_groups=mesh['seg'=32,'pair'=4] {'seg','pair'}, dimensions={0} | all-to-all | bytes 131072 | tf_op jit(solution)/shard_map/all_to_all | solution.py:370
  91.0 0.0 copy-done
  91.0 0.9 %answer.1 = (f32[768]{0:T(1024)}, f32[768]{0:T(1024)}) custom-call(f32[128,128]{1,0:T(8,128)S(1)} %bitcast.8, s32[8,768]{1,0:T(8,128)S(1)} %copy-done), custom_call_target="tpu_custom_call" | custom-call | bytes 90112 | tf_op jit(solution)/shard_map/answer/pallas_call | solution.py:315
  (1 shorter events, 0.0 us)
Async XLA Ops:
  46.5 16.9 %collective-permute-start.1 = (bf16[784,768]{1,0:T(8,128)(2,1)S(1)}, bf16[784,768]{1,0:T(8,128)(2,1)S(1)}, u32[]{:S(2)}, u32[]{:S(2)}) collective-permute-start(bf16[784,768]{1,0:T(8,128)(2,1)S(1)} %get-tuple-element.7.own_ref), channel_id=1, source_target_pairs={{82,83},{83,17},{17,87},{87,21},{21,91},{91,25},{25,107},{107,41},... | collective-permute-start | bytes 3612680 | tf_op jit(solution)/shard_map/ppermute | solution.py:354
  46.8 18.1 %collective-permute-start.2 = (bf16[400,768]{1,0:T(8,128)(2,1)S(1)}, bf16[400,768]{1,0:T(8,128)(2,1)S(1)}, u32[]{:S(2)}, u32[]{:S(2)}) collective-permute-start(bf16[400,768]{1,0:T(8,128)(2,1)S(1)} %slice.3), channel_id=1, source_target_pairs={{18,83},{82,17},{83,87},{17,21},{87,91},{21,25},{91,107},{25,41},{... | collective-permute-start | bytes 1843208 | tf_op jit(solution)/shard_map/ppermute | solution.py:356
  48.1 16.8 %collective-permute-start.3 = (bf16[400,768]{1,0:T(8,128)(2,1)S(1)}, bf16[400,768]{1,0:T(8,128)(2,1)S(1)}, u32[]{:S(2)}, u32[]{:S(2)}) collective-permute-start(bf16[400,768]{1,0:T(8,128)(2,1)S(1)} %get-tuple-element.8), channel_id=1, source_target_pairs={{87,83},{21,17},{91,87},{25,21},{107,91},{41,25},{111,107},{45,41}... | collective-permute-start | bytes 1843208 | tf_op jit(solution)/shard_map/ppermute | solution.py:355
  49.5 17.2 %collective-permute-start = (bf16[400,768]{1,0:T(8,128)(2,1)S(1)}, bf16[400,768]{1,0:T(8,128)(2,1)S(1)}, u32[]{:S(2)}, u32[]{:S(2)}) collective-permute-start(bf16[400,768]{1,0:T(8,128)(2,1)S(1)} %slice.3), channel_id=1, source_target_pairs={{87,83},{21,17},{91,87},{25,21},{107,91},{41,25},{111,107},{45,41}... | collective-permute-start | bytes 1843208 | tf_op jit(solution)/shard_map/ppermute | solution.py:357
  66.7 24.3 %copy-start = (s32[8,768]{1,0:T(8,128)S(1)}, s32[8,768]{1,0:T(8,128)}, u32[]{:S(2)}) copy-start(s32[8,768]{1,0:T(8,128)} %get-tuple-element.9.route_ref) | copy-start | bytes 73732

commit v4 on v3

--- a/solution.py
+++ b/solution.py
@@ -27,6 +27,7 @@
 ]
 ROWS = 768
 HALF = 384
+EARLY = 512
 CAP = 9
 SLOTS = DEVICES * CAP
 MAIN = DEVICES * 8
@@ -144,8 +145,8 @@
     out_ref[ROWS + 9 : ROWS + 10, :] = cols[1:2, :ROWS]
     out_ref[ROWS + 10 : ROWS + 11, :HALF] = cols[0:1, ROWS:]
     out_ref[ROWS + 11 : ROWS + 12, :HALF] = cols[1:2, ROWS:]
-    first_ref[:HALF, :] = out_ref[:HALF, :]
-    first_ref[HALF:, :] = out_ref[ROWS:, :]
+    first_ref[:EARLY, :] = out_ref[:EARLY, :]
+    first_ref[EARLY:, :] = out_ref[ROWS:, :]
 
 
 def read_meta(block_ref, rows):
@@ -182,18 +183,22 @@
 
 def meet(key, ids, others):
     cid, rank = columns(*ids)
-    key_all = jnp.full((HALF, 128), -1.0, F32)
+    rows = key.shape[0]
+    key_all = jnp.full((rows, 128), -1.0, F32)
     key_high, found = key_all, []
     for ref, count, other_cid, other_rank in others:
-        wide_all, wide_high, row_all, row_high = against(key, cid, rank, ref, count, other_cid, other_rank)
+        near = HALF if count == HALF else rows
+        wide_all, wide_high, row_all, row_high = against(key[:near], cid[:near], rank[:near], ref, count, other_cid, other_rank)
+        if near < rows:
+            rest = jnp.full((rows - near, 128), -1.0, F32)
+            wide_all, wide_high = jnp.concatenate([wide_all, rest], axis=0), jnp.concatenate([wide_high, rest], axis=0)
         key_all, key_high = jnp.maximum(key_all, wide_all), jnp.maximum(key_high, wide_high)
         found.append((row_all, row_high))
     return tuple(jnp.max(jnp.transpose(wide), axis=0, keepdims=True) for wide in (key_all, key_high)), found
 
 
-def half_ids(ids, half):
-    part = slice(half * HALF, (half + 1) * HALF)
-    return ids[0][:, part], ids[1][:, part]
+def ids_of(ids, start, stop):
+    return ids[0][:, start:stop], ids[1][:, start:stop]
 
 
 def both(left, right):
@@ -245,7 +250,7 @@
     mine, theirs = [], None
     for half in range(2):
         rows = own_ref[half * HALF : (half + 1) * HALF, :]
-        keys, (found,) = meet(rows, half_ids(own, half), [(mate_ref, ROWS, *mate[:2])])
+        keys, (found,) = meet(rows, ids_of(own, half * HALF, half * HALF + HALF), [(mate_ref, ROWS, *mate[:2])])
         mine.append(keys)
         theirs = found if theirs is None else both(theirs, found)
     mine = [jnp.concatenate([mine[0][i], mine[1][i]], axis=1) for i in range(2)]
@@ -255,28 +260,29 @@
 
 def far_first_kernel(key_ref, own_ref, mate_ref, tail_ref, near_ref, out_ref):
     own, mate = read_meta(own_ref, ROWS), read_meta(mate_ref, ROWS)
-    key, tail = read_meta(key_ref, HALF), read_meta(tail_ref, HALF)
+    key, tail = read_meta(key_ref, EARLY), read_meta(tail_ref, HALF)
     keys, (tails, mates, owns) = meet(
-        key_ref[:HALF, :],
-        half_ids(key, 0),
-        [(tail_ref, HALF, *half_ids(tail, 1)), (mate_ref, ROWS, *mate[:2]), (own_ref, ROWS, *own[:2])],
+        key_ref[:EARLY, :],
+        ids_of(key, 0, EARLY),
+        [(tail_ref, HALF, *ids_of(tail, HALF, ROWS)), (mate_ref, ROWS, *mate[:2]), (own_ref, ROWS, *own[:2])],
     )
     owns = both(owns, (near_ref[0:1, :], near_ref[1:2, :]))
     mates = both(mates, (near_ref[2:3, :], near_ref[3:4, :]))
-    ends = [jnp.concatenate([keys[i], tails[i]], axis=1) for i in range(2)]
-    out_ref[...] = jnp.concatenate([*owns, *mates, *ends, jnp.zeros((2, ROWS), F32)], axis=0)
-
-
-def far_second_kernel(key_ref, own_ref, mate_ref, tail_ref, first_ref, out_ref, by_slot):
+    lines = [jnp.concatenate([keys[i], jnp.zeros((1, ROWS - EARLY), F32)], axis=1) for i in range(2)]
+    lines += [jnp.concatenate([tails[i], jnp.zeros((1, HALF), F32)], axis=1) for i in range(2)]
+    out_ref[...] = jnp.concatenate([*owns, *mates, *lines], axis=0)
+
+
+def far_second_kernel(key_ref, own_ref, mate_ref, early_ref, tail_ref, first_ref, out_ref, by_slot):
     own, mate = read_meta(own_ref, ROWS), read_meta(mate_ref, ROWS)
-    key, tail = read_meta(key_ref, HALF), read_meta(tail_ref, HALF)
+    key, tail = read_meta(early_ref, EARLY), read_meta(tail_ref, HALF)
     keys, (mates, owns) = meet(
-        key_ref[:HALF, :], half_ids(key, 1), [(mate_ref, ROWS, *mate[:2]), (own_ref, ROWS, *own[:2])]
-    )
-    line = [first_ref[i : i + 1, :] for i in range(6)]
+        key_ref[...], ids_of(key, EARLY, ROWS), [(mate_ref, ROWS, *mate[:2]), (own_ref, ROWS, *own[:2])]
+    )
+    line = [first_ref[i : i + 1, :] for i in range(8)]
     owns, mates = both(owns, line[0:2]), both(mates, line[2:4])
-    keys = [jnp.concatenate([line[4 + i][:, :HALF], keys[i]], axis=1) for i in range(2)]
-    tails = [line[4 + i][:, HALF:] for i in range(2)]
+    keys = [jnp.concatenate([line[4 + i][:, :EARLY], keys[i]], axis=1) for i in range(2)]
+    tails = [line[6 + i][:, :HALF] for i in range(2)]
     rows = []
     for part, slot in ((owns, own[2]), (mates, mate[2]), (keys, key[2]), (tails, tail[2] - HALF)):
         rows += reply_to(*part, slot)
@@ -345,16 +351,15 @@
     got = lax.all_to_all(send, AXES, split_axis=0, concat_axis=0, tiled=True)
     own, first = call(
         unpack_kernel,
-        [((ROWS + META, ROWS), BF), ((HALF + META, ROWS), BF)],
+        [((ROWS + META, ROWS), BF), ((EARLY + META, ROWS), BF)],
         (got,),
         (pltpu.VMEM((MAIN, 128), F32), pltpu.VMEM((MAIN, 128), F32)),
         name="unpack",
     )
-    second = own[HALF:]
     mate = lax.ppermute(own, AXES, shift(-1))
     key1 = lax.ppermute(first, AXES, shift(2))
-    tail = lax.ppermute(second, AXES, shift(-2))
-    key2 = lax.ppermute(second, AXES, shift(2))
+    tail = lax.ppermute(own[HALF:], AXES, shift(-2))
+    key2 = lax.ppermute(own[EARLY:ROWS], AXES, shift(2))
     tile = 2 * ROWS**3
     local = call(local_kernel, ((8, ROWS), F32), (own,), flops=tile, name="local")
     near = call(mate_kernel, ((8, ROWS), F32), (own, mate, local), flops=tile, name="mate")
@@ -362,7 +367,7 @@
     reply = call(
         far_second_kernel,
         ((DEVICES, 128), F32),
-        (key2, own, mate, tail, lines),
+        (key2, own, mate, key1, tail, lines),
         (pltpu.VMEM((SLOTS, 128), F32),),
         flops=tile,
         name="far_second",

time: 92.2 us -> 91.5 us (level)
    ppermute x1, starting transfers between devices: 1.41 us -> 2.5 us  [body(): key1 = lax.ppermute(first, AXES, shift(2))]
  transfers between devices with their start and end apart: 4 -> 4, of which waited for: 1 -> 1; matrix products, arithmetic and copies ran while one was open for 0% -> 0% of each run, Pallas kernels for 5% -> 6%
where the time goes in v4:
time: 91.5 us; the launch traced here: 91.2 us
  blocking collectives  60.3 us (66%)
  Pallas kernels  14.8 us (16%)
  waiting for transfers between devices  9.62 us (11%)
  starting transfers between devices  5.75 us (6%)
    all_to_all x1, blocking collectives, body(): got = lax.all_to_all(send, AXES, split_axis=0, concat_axis=0, tiled=True)  39 us
    all_to_all x1, blocking collectives, body(): lax.all_to_all(reply.reshape(DEVICES, 1, 128), AXES, split_axis=0, concat...  21.3 us
    pallas_call x7, Pallas kernels, call(): pl.pallas_call(kernel, out_shape=shapes if many else shapes[0], in_specs=...  14.8 us
    ppermute x1, waiting for transfers between devices, body(): mate = lax.ppermute(own, AXES, shift(-1))  9.61 us
    ppermute x1, starting transfers between devices, body(): key2 = lax.ppermute(own[EARLY:ROWS], AXES, shift(2))  2.91 us
    ppermute x1, starting transfers between devices, body(): key1 = lax.ppermute(first, AXES, shift(2))  2.5 us
  transfers between devices with their start and end apart: 4, of which 1 were waited for; matrix products, arithmetic and copies ran while one was open for 0% of the time, Pallas kernels for 6%

profile of v4, /device:TPU:1, one launch (start us, length us, event | category | flops | bytes accessed | tf_op | source)
XLA Modules:
  0.0 91.2 jit_solution(3657080846536435407)
XLA Ops:
  0.6 4.5 %pack.1 = (bf16[1024,896]{1,0:T(8,128)(2,1)}, s32[8,768]{1,0:T(8,128)}) custom-call(bf16[768,768]{1,0:T(8,128)(2,1)} %emb_ref.1, s32[768]{0:T(1024)} %cid_ref.1, s32[768]{0:T(1024)} %rank_ref.1, s32[768]{0:T(1024)} %slot_ref.1), custom_call_target="tpu_custom_call" | custom-call | bytes 1188864 | tf_op jit(solution)/shard_map/pack/pallas_call | solution.py:321
  5.1 39.0 %all_to_all.16 = bf16[128,8,896]{2,1,0:T(8,128)(2,1)S(1)} all-to-all(bf16[128,8,896]{2,1,0:T(8,128)(2,1)} %bitcast.9), channel_id=1, replica_groups=mesh['seg'=32,'pair'=4] {'seg','pair'}, dimensions={0} | all-to-all | bytes 3670016 | tf_op jit(solution)/shard_map/all_to_all | solution.py:351
  44.1 2.3 %unpack.1 = (bf16[784,768]{1,0:T(8,128)(2,1)S(1)}, bf16[528,768]{1,0:T(8,128)(2,1)S(1)}) custom-call(bf16[1024,896]{1,0:T(8,128)(2,1)S(1)} %bitcast.6), custom_call_target="tpu_custom_call" | custom-call | bytes 1835008 | tf_op jit(solution)/shard_map/unpack/pallas_call | solution.py:321
  46.5 0.3 collective-permute-start.1
  46.7 2.5 %collective-permute-start.2 = (bf16[528,768]{1,0:T(8,128)(2,1)S(1)}, bf16[528,768]{1,0:T(8,128)(2,1)S(1)}, u32[]{:S(2)}, u32[]{:S(2)}) collective-permute-start(bf16[528,768]{1,0:T(8,128)(2,1)S(1)} %get-tuple-element.8), channel_id=1, source_target_pairs={{87,83},{21,17},{91,87},{25,21},{107,91},{41,25},{111,107},{45,41}... | collective-permute-start | bytes 2433032 | tf_op jit(solution)/shard_map/ppermute | solution.py:360
  49.3 0.1 collective-permute-start.3
  49.4 2.9 %collective-permute-start = (bf16[256,768]{1,0:T(8,128)(2,1)S(1)}, bf16[256,768]{1,0:T(8,128)(2,1)S(1)}, u32[]{:S(2)}, u32[]{:S(2)}) collective-permute-start(bf16[256,768]{1,0:T(8,128)(2,1)S(1)} %slice.6), channel_id=1, source_target_pairs={{87,83},{21,17},{91,87},{25,21},{107,91},{41,25},{111,107},{45,41}... | collective-permute-start | bytes 1179656 | tf_op jit(solution)/shard_map/ppermute | solution.py:362
  52.3 1.4 %local.1.local_ref = f32[8,768]{1,0:T(8,128)S(1)} custom-call(bf16[784,768]{1,0:T(8,128)(2,1)S(1)} %get-tuple-element.7.own_ref), custom_call_target="tpu_custom_call" | custom-call | flops 905969664 | bytes 1204224 | tf_op jit(solution)/shard_map/local/pallas_call | solution.py:321
  53.7 9.6 %collective-permute-done.1.mate_ref = bf16[784,768]{1,0:T(8,128)(2,1)S(1)} collective-permute-done((bf16[784,768]{1,0:T(8,128)(2,1)S(1)}, bf16[784,768]{1,0:T(8,128)(2,1)S(1)}, u32[]{:S(2)}, u32[]{:S(2)}) %collective-permute-start.1) | collective-permute-done | bytes 1204256 | tf_op jit(solution)/shard_map/ppermute | solution.py:359
  63.4 1.5 %mate.1.near_ref = f32[8,768]{1,0:T(8,128)S(1)} custom-call(bf16[784,768]{1,0:T(8,128)(2,1)S(1)} %get-tuple-element.7.own_ref, bf16[784,768]{1,0:T(8,128)(2,1)S(1)} %collective-permute-done.1.mate_ref, f32[8,768]{1,0:T(8,128)S(1)} %local.1.local_ref), custom_call_target="tpu_custom_call" | custom-call | flops 905969664 | bytes 2433024 | tf_op jit(solution)/shard_map/mate/pallas_call | solution.py:321
  64.9 0.0 collective-permute-done.3.tail_ref
  64.9 0.0 collective-permute-done.2.key_ref.early_ref
  64.9 2.3 %far_first.1.first_ref = f32[8,768]{1,0:T(8,128)S(1)} custom-call(bf16[528,768]{1,0:T(8,128)(2,1)S(1)} %collective-permute-done.2.key_ref.early_ref, bf16[784,768]{1,0:T(8,128)(2,1)S(1)} %get-tuple-element.7.own_ref, bf16[784,768]{1,0:T(8,128)(2,1)S(1)} %collective-permute-done.1.mate_ref, bf16[400,768]{1,0:T(8,128)(2,1)S(1)} %collective-permute-done.3.tail_ref, ...), custom_call_target="tpu_custom_call" | custom-call | flops 905969664 | bytes 3858432 | tf_op jit(solution)/shard_map/far_first/pallas_call | solution.py:321
  67.2 0.0 copy-start
  67.2 0.0 collective-permute-done.key_ref
  67.2 1.8 %far_second.1 = f32[128,128]{1,0:T(8,128)S(1)} custom-call(bf16[256,768]{1,0:T(8,128)(2,1)S(1)} %collective-permute-done.key_ref, bf16[784,768]{1,0:T(8,128)(2,1)S(1)} %get-tuple-element.7.own_ref, bf16[784,768]{1,0:T(8,128)(2,1)S(1)} %collective-permute-done.1.mate_ref, bf16[528,768]{1,0:T(8,128)(2,1)S(1)} %collective-permute-done.2.key_ref.early_ref, ...), custom_call_target="tpu_custom_call" | custom-call | flops 905969664 | bytes 4251648 | tf_op jit(solution)/shard_map/far_second/pallas_call | solution.py:321
  69.0 21.3 %all_to_all.17 = f32[128,1,128]{2,1,0:T(1,128)S(1)} all-to-all(f32[128,1,128]{2,1,0:T(1,128)S(1)} %bitcast.7), channel_id=1, replica_groups=mesh['seg'=32,'pair'=4] {'seg','pair'}, dimensions={0} | all-to-all | bytes 131072 | tf_op jit(solution)/shard_map/all_to_all | solution.py:375
  90.3 0.0 copy-done
  90.3 0.9 %answer.1 = (f32[768]{0:T(1024)}, f32[768]{0:T(1024)}) custom-call(f32[128,128]{1,0:T(8,128)S(1)} %bitcast.8, s32[8,768]{1,0:T(8,128)S(1)} %copy-done), custom_call_target="tpu_custom_call" | custom-call | bytes 90112 | tf_op jit(solution)/shard_map/answer/pallas_call | solution.py:321
  (2 shorter events, 0.1 us)
Async XLA Ops:
  46.5 16.9 %collective-permute-start.1 = (bf16[784,768]{1,0:T(8,128)(2,1)S(1)}, bf16[784,768]{1,0:T(8,128)(2,1)S(1)}, u32[]{:S(2)}, u32[]{:S(2)}) collective-permute-start(bf16[784,768]{1,0:T(8,128)(2,1)S(1)} %get-tuple-element.7.own_ref), channel_id=1, source_target_pairs={{82,83},{83,17},{17,87},{87,21},{21,91},{91,25},{25,107},{107,41},... | collective-permute-start | bytes 3612680 | tf_op jit(solution)/shard_map/ppermute | solution.py:359
  46.7 18.2 %collective-permute-start.2 = (bf16[528,768]{1,0:T(8,128)(2,1)S(1)}, bf16[528,768]{1,0:T(8,128)(2,1)S(1)}, u32[]{:S(2)}, u32[]{:S(2)}) collective-permute-start(bf16[528,768]{1,0:T(8,128)(2,1)S(1)} %get-tuple-element.8), channel_id=1, source_target_pairs={{87,83},{21,17},{91,87},{25,21},{107,91},{41,25},{111,107},{45,41}... | collective-permute-start | bytes 2433032 | tf_op jit(solution)/shard_map/ppermute | solution.py:360
  49.3 15.6 %collective-permute-start.3 = (bf16[400,768]{1,0:T(8,128)(2,1)S(1)}, bf16[400,768]{1,0:T(8,128)(2,1)S(1)}, u32[]{:S(2)}, u32[]{:S(2)}) collective-permute-start(bf16[400,768]{1,0:T(8,128)(2,1)S(1)} %slice.7), channel_id=1, source_target_pairs={{18,83},{82,17},{83,87},{17,21},{87,91},{21,25},{91,107},{25,41},{... | collective-permute-start | bytes 1843208 | tf_op jit(solution)/shard_map/ppermute | solution.py:361
  49.4 17.8 %collective-permute-start = (bf16[256,768]{1,0:T(8,128)(2,1)S(1)}, bf16[256,768]{1,0:T(8,128)(2,1)S(1)}, u32[]{:S(2)}, u32[]{:S(2)}) collective-permute-start(bf16[256,768]{1,0:T(8,128)(2,1)S(1)} %slice.6), channel_id=1, source_target_pairs={{87,83},{21,17},{91,87},{25,21},{107,91},{41,25},{111,107},{45,41}... | collective-permute-start | bytes 1179656 | tf_op jit(solution)/shard_map/ppermute | solution.py:362
  67.2 23.1 %copy-start = (s32[8,768]{1,0:T(8,128)S(1)}, s32[8,768]{1,0:T(8,128)}, u32[]{:S(2)}) copy-start(s32[8,768]{1,0:T(8,128)} %get-tuple-element.9.route_ref) | copy-start | bytes 73732

commit v5 on v4

--- a/solution.py
+++ b/solution.py
@@ -258,7 +258,7 @@
     out_ref[...] = jnp.concatenate([*mine, *theirs, jnp.full((4, ROWS), -1.0, F32)], axis=0)
 
 
-def far_first_kernel(key_ref, own_ref, mate_ref, tail_ref, near_ref, out_ref):
+def far_first_kernel(key_ref, own_ref, mate_ref, tail_ref, near_ref, out_ref, tail_rows_ref):
     own, mate = read_meta(own_ref, ROWS), read_meta(mate_ref, ROWS)
     key, tail = read_meta(key_ref, EARLY), read_meta(tail_ref, HALF)
     keys, (tails, mates, owns) = meet(
@@ -269,24 +269,23 @@
     owns = both(owns, (near_ref[0:1, :], near_ref[1:2, :]))
     mates = both(mates, (near_ref[2:3, :], near_ref[3:4, :]))
     lines = [jnp.concatenate([keys[i], jnp.zeros((1, ROWS - EARLY), F32)], axis=1) for i in range(2)]
-    lines += [jnp.concatenate([tails[i], jnp.zeros((1, HALF), F32)], axis=1) for i in range(2)]
-    out_ref[...] = jnp.concatenate([*owns, *mates, *lines], axis=0)
-
-
-def far_second_kernel(key_ref, own_ref, mate_ref, early_ref, tail_ref, first_ref, out_ref, by_slot):
+    out_ref[...] = jnp.concatenate([*owns, *mates, *lines, jnp.zeros((2, ROWS), F32)], axis=0)
+    tail_rows_ref[...] = jnp.concatenate(reply_to(*tails, tail[2] - HALF), axis=0)
+
+
+def far_second_kernel(key_ref, own_ref, mate_ref, early_ref, first_ref, tail_rows_ref, out_ref, by_slot):
     own, mate = read_meta(own_ref, ROWS), read_meta(mate_ref, ROWS)
-    key, tail = read_meta(early_ref, EARLY), read_meta(tail_ref, HALF)
+    key = read_meta(early_ref, EARLY)
     keys, (mates, owns) = meet(
         key_ref[...], ids_of(key, EARLY, ROWS), [(mate_ref, ROWS, *mate[:2]), (own_ref, ROWS, *own[:2])]
     )
-    line = [first_ref[i : i + 1, :] for i in range(8)]
+    line = [first_ref[i : i + 1, :] for i in range(6)]
     owns, mates = both(owns, line[0:2]), both(mates, line[2:4])
     keys = [jnp.concatenate([line[4 + i][:, :EARLY], keys[i]], axis=1) for i in range(2)]
-    tails = [line[6 + i][:, :HALF] for i in range(2)]
     rows = []
-    for part, slot in ((owns, own[2]), (mates, mate[2]), (keys, key[2]), (tails, tail[2] - HALF)):
+    for part, slot in ((owns, own[2]), (mates, mate[2]), (keys, key[2])):
         rows += reply_to(*part, slot)
-    rows.append(jnp.zeros((32, SLOTS), F32))
+    rows += [tail_rows_ref[...], jnp.zeros((32, SLOTS), F32)]
     by_slot[...] = jnp.transpose(jnp.concatenate(rows, axis=0))
     reply = by_slot[pl.ds(0, DEVICES, stride=8), :]
     for order in range(1, 8):
@@ -363,11 +362,17 @@
     tile = 2 * ROWS**3
     local = call(local_kernel, ((8, ROWS), F32), (own,), flops=tile, name="local")
     near = call(mate_kernel, ((8, ROWS), F32), (own, mate, local), flops=tile, name="mate")
-    lines = call(far_first_kernel, ((8, ROWS), F32), (key1, own, mate, tail, near), flops=tile, name="far_first")
+    lines, tail_rows = call(
+        far_first_kernel,
+        [((8, ROWS), F32), ((24, SLOTS), F32)],
+        (key1, own, mate, tail, near),
+        flops=tile,
+        name="far_first",
+    )
     reply = call(
         far_second_kernel,
         ((DEVICES, 128), F32),
-        (key2, own, mate, key1, tail, lines),
+        (key2, own, mate, key1, lines, tail_rows),
         (pltpu.VMEM((SLOTS, 128), F32),),
         flops=tile,
         name="far_second",

time: 91.5 us -> 91.4 us (level)
  no operation moved by 1% of the time
where the time goes in v5:
time: 91.4 us; the launch traced here: 91.2 us
  blocking collectives  60.3 us (66%)
  Pallas kernels  14.7 us (16%)
  waiting for transfers between devices  9.65 us (11%)
  starting transfers between devices  5.75 us (6%)
    all_to_all x1, blocking collectives, body(): got = lax.all_to_all(send, AXES, split_axis=0, concat_axis=0, tiled=True)  39 us
    all_to_all x1, blocking collectives, body(): lax.all_to_all(reply.reshape(DEVICES, 1, 128), AXES, split_axis=0, concat...  21.3 us
    pallas_call x7, Pallas kernels, call(): pl.pallas_call(kernel, out_shape=shapes if many else shapes[0], in_specs=...  14.7 us
    ppermute x1, waiting for transfers between devices, body(): mate = lax.ppermute(own, AXES, shift(-1))  9.64 us
    ppermute x1, starting transfers between devices, body(): key2 = lax.ppermute(own[EARLY:ROWS], AXES, shift(2))  2.91 us
    ppermute x1, starting transfers between devices, body(): key1 = lax.ppermute(first, AXES, shift(2))  2.5 us
  transfers between devices with their start and end apart: 4, of which 1 were waited for; matrix products, arithmetic and copies ran while one was open for 0% of the time, Pallas kernels for 6%

profile of v5, /device:TPU:1, one launch (start us, length us, event | category | flops | bytes accessed | tf_op | source)
XLA Modules:
  0.0 91.2 jit_solution(8445973029385524415)
XLA Ops:
  0.6 4.5 %pack.1 = (bf16[1024,896]{1,0:T(8,128)(2,1)}, s32[8,768]{1,0:T(8,128)}) custom-call(bf16[768,768]{1,0:T(8,128)(2,1)} %emb_ref.1, s32[768]{0:T(1024)} %cid_ref.1, s32[768]{0:T(1024)} %rank_ref.1, s32[768]{0:T(1024)} %slot_ref.1), custom_call_target="tpu_custom_call" | custom-call | bytes 1188864 | tf_op jit(solution)/shard_map/pack/pallas_call | solution.py:320
  5.1 39.0 %all_to_all.16 = bf16[128,8,896]{2,1,0:T(8,128)(2,1)S(1)} all-to-all(bf16[128,8,896]{2,1,0:T(8,128)(2,1)} %bitcast.9), channel_id=1, replica_groups=mesh['seg'=32,'pair'=4] {'seg','pair'}, dimensions={0} | all-to-all | bytes 3670016 | tf_op jit(solution)/shard_map/all_to_all | solution.py:350
  44.1 2.3 %unpack.1 = (bf16[784,768]{1,0:T(8,128)(2,1)S(1)}, bf16[528,768]{1,0:T(8,128)(2,1)S(1)}) custom-call(bf16[1024,896]{1,0:T(8,128)(2,1)S(1)} %bitcast.6), custom_call_target="tpu_custom_call" | custom-call | bytes 1835008 | tf_op jit(solution)/shard_map/unpack/pallas_call | solution.py:320
  46.5 0.3 collective-permute-start.1
  46.7 2.5 %collective-permute-start.2 = (bf16[528,768]{1,0:T(8,128)(2,1)S(1)}, bf16[528,768]{1,0:T(8,128)(2,1)S(1)}, u32[]{:S(2)}, u32[]{:S(2)}) collective-permute-start(bf16[528,768]{1,0:T(8,128)(2,1)S(1)} %get-tuple-element.10), channel_id=1, source_target_pairs={{87,83},{21,17},{91,87},{25,21},{107,91},{41,25},{111,107},{45,41}... | collective-permute-start | bytes 2433032 | tf_op jit(solution)/shard_map/ppermute | solution.py:359
  49.3 0.1 collective-permute-start.3
  49.4 2.9 %collective-permute-start = (bf16[256,768]{1,0:T(8,128)(2,1)S(1)}, bf16[256,768]{1,0:T(8,128)(2,1)S(1)}, u32[]{:S(2)}, u32[]{:S(2)}) collective-permute-start(bf16[256,768]{1,0:T(8,128)(2,1)S(1)} %slice.6), channel_id=1, source_target_pairs={{87,83},{21,17},{91,87},{25,21},{107,91},{41,25},{111,107},{45,41}... | collective-permute-start | bytes 1179656 | tf_op jit(solution)/shard_map/ppermute | solution.py:361
  52.3 1.4 %local.1.local_ref = f32[8,768]{1,0:T(8,128)S(1)} custom-call(bf16[784,768]{1,0:T(8,128)(2,1)S(1)} %get-tuple-element.9.own_ref), custom_call_target="tpu_custom_call" | custom-call | flops 905969664 | bytes 1204224 | tf_op jit(solution)/shard_map/local/pallas_call | solution.py:320
  53.7 9.6 %collective-permute-done.1.mate_ref = bf16[784,768]{1,0:T(8,128)(2,1)S(1)} collective-permute-done((bf16[784,768]{1,0:T(8,128)(2,1)S(1)}, bf16[784,768]{1,0:T(8,128)(2,1)S(1)}, u32[]{:S(2)}, u32[]{:S(2)}) %collective-permute-start.1) | collective-permute-done | bytes 1204256 | tf_op jit(solution)/shard_map/ppermute | solution.py:358
  63.4 1.5 %mate.1.near_ref = f32[8,768]{1,0:T(8,128)S(1)} custom-call(bf16[784,768]{1,0:T(8,128)(2,1)S(1)} %get-tuple-element.9.own_ref, bf16[784,768]{1,0:T(8,128)(2,1)S(1)} %collective-permute-done.1.mate_ref, f32[8,768]{1,0:T(8,128)S(1)} %local.1.local_ref), custom_call_target="tpu_custom_call" | custom-call | flops 905969664 | bytes 2433024 | tf_op jit(solution)/shard_map/mate/pallas_call | solution.py:320
  64.8 0.0 collective-permute-done.3.tail_ref
  64.9 0.0 collective-permute-done.2.key_ref.early_ref
  64.9 2.3 %far_first.1 = (f32[8,768]{1,0:T(8,128)S(1)}, f32[24,1152]{1,0:T(8,128)S(1)}) custom-call(bf16[528,768]{1,0:T(8,128)(2,1)S(1)} %collective-permute-done.2.key_ref.early_ref, bf16[784,768]{1,0:T(8,128)(2,1)S(1)} %get-tuple-element.9.own_ref, bf16[784,768]{1,0:T(8,128)(2,1)S(1)} %collective-permute-done.1.mate_ref, ...), custom_call_target="tpu_custom_call" | custom-call | flops 905969664 | bytes 3858432 | tf_op jit(solution)/shard_map/far_first/pallas_call | solution.py:320
  67.2 0.0 collective-permute-done.key_ref
  67.2 0.0 copy-start
  67.2 1.8 %far_second.1 = f32[128,128]{1,0:T(8,128)S(1)} custom-call(bf16[256,768]{1,0:T(8,128)(2,1)S(1)} %collective-permute-done.key_ref, bf16[784,768]{1,0:T(8,128)(2,1)S(1)} %get-tuple-element.9.own_ref, bf16[784,768]{1,0:T(8,128)(2,1)S(1)} %collective-permute-done.1.mate_ref, bf16[528,768]{1,0:T(8,128)(2,1)S(1)} %collective-permute-done.2.key_ref.early_ref, ...), custom_call_target="tpu_custom_call" | custom-call | flops 905969664 | bytes 3747840 | tf_op jit(solution)/shard_map/far_second/pallas_call | solution.py:320
  69.0 21.3 %all_to_all.17 = f32[128,1,128]{2,1,0:T(1,128)S(1)} all-to-all(f32[128,1,128]{2,1,0:T(1,128)S(1)} %bitcast.7), channel_id=1, replica_groups=mesh['seg'=32,'pair'=4] {'seg','pair'}, dimensions={0} | all-to-all | bytes 131072 | tf_op jit(solution)/shard_map/all_to_all | solution.py:380
  90.2 0.0 copy-done
  90.2 0.9 %answer.1 = (f32[768]{0:T(1024)}, f32[768]{0:T(1024)}) custom-call(f32[128,128]{1,0:T(8,128)S(1)} %bitcast.8, s32[8,768]{1,0:T(8,128)S(1)} %copy-done), custom_call_target="tpu_custom_call" | custom-call | bytes 90112 | tf_op jit(solution)/shard_map/answer/pallas_call | solution.py:320
  (2 shorter events, 0.1 us)
Async XLA Ops:
  46.5 16.9 %collective-permute-start.1 = (bf16[784,768]{1,0:T(8,128)(2,1)S(1)}, bf16[784,768]{1,0:T(8,128)(2,1)S(1)}, u32[]{:S(2)}, u32[]{:S(2)}) collective-permute-start(bf16[784,768]{1,0:T(8,128)(2,1)S(1)} %get-tuple-element.9.own_ref), channel_id=1, source_target_pairs={{82,83},{83,17},{17,87},{87,21},{21,91},{91,25},{25,107},{107,41},... | collective-permute-start | bytes 3612680 | tf_op jit(solution)/shard_map/ppermute | solution.py:358
  46.7 18.1 %collective-permute-start.2 = (bf16[528,768]{1,0:T(8,128)(2,1)S(1)}, bf16[528,768]{1,0:T(8,128)(2,1)S(1)}, u32[]{:S(2)}, u32[]{:S(2)}) collective-permute-start(bf16[528,768]{1,0:T(8,128)(2,1)S(1)} %get-tuple-element.10), channel_id=1, source_target_pairs={{87,83},{21,17},{91,87},{25,21},{107,91},{41,25},{111,107},{45,41}... | collective-permute-start | bytes 2433032 | tf_op jit(solution)/shard_map/ppermute | solution.py:359
  49.3 15.6 %collective-permute-start.3 = (bf16[400,768]{1,0:T(8,128)(2,1)S(1)}, bf16[400,768]{1,0:T(8,128)(2,1)S(1)}, u32[]{:S(2)}, u32[]{:S(2)}) collective-permute-start(bf16[400,768]{1,0:T(8,128)(2,1)S(1)} %slice.7), channel_id=1, source_target_pairs={{18,83},{82,17},{83,87},{17,21},{87,91},{21,25},{91,107},{25,41},{... | collective-permute-start | bytes 1843208 | tf_op jit(solution)/shard_map/ppermute | solution.py:360
  49.4 17.8 %collective-permute-start = (bf16[256,768]{1,0:T(8,128)(2,1)S(1)}, bf16[256,768]{1,0:T(8,128)(2,1)S(1)}, u32[]{:S(2)}, u32[]{:S(2)}) collective-permute-start(bf16[256,768]{1,0:T(8,128)(2,1)S(1)} %slice.6), channel_id=1, source_target_pairs={{87,83},{21,17},{91,87},{25,21},{107,91},{41,25},{111,107},{45,41}... | collective-permute-start | bytes 1179656 | tf_op jit(solution)/shard_map/ppermute | solution.py:361
  67.2 23.0 %copy-start = (s32[8,768]{1,0:T(8,128)S(1)}, s32[8,768]{1,0:T(8,128)}, u32[]{:S(2)}) copy-start(s32[8,768]{1,0:T(8,128)} %get-tuple-element.13.route_ref) | copy-start | bytes 73732

commit v6 on v4

--- a/solution.py
+++ b/solution.py
@@ -100,6 +100,13 @@
     device = senders[0:1]
     to_device = (iota((DEVICES, ROWS), 0) == device).astype(BF)
     flat = jnp.where(within < 8, device * 8 + within, -1)
+    field = iota((DEVICES, ROWS), 0) >> 4
+    meta = jnp.where(field == 0, (local >> 8) + 1, jnp.where(field == 1, local & 255, jnp.where(field == 2, cid + 1, 0)))
+    meta = jnp.where(field == 3, rank >> 8, jnp.where(field == 4, rank & 255, meta))
+    meta = jnp.where((iota((DEVICES, ROWS), 0) & 15) == within, meta, 0).astype(F32).astype(BF)
+    extra[...] = jnp.zeros_like(extra)
+    extra[pl.ds(6, DEVICES, stride=8), :] = dot_nt(to_device, meta)
+    ninth = jnp.where(within == 8, to_device, jnp.zeros_like(to_device))
     for part, copy in enumerate(copies):
         copy.wait()
         values = raw[part * 256 : (part + 1) * 256, :].astype(F32)
@@ -108,16 +115,9 @@
     for start in range(0, MAIN, 256):
         pick = (iota((256, ROWS), 0) + start == flat).astype(BF)
         out_ref[start : start + 256, :ROWS] = dot(pick, unit[...]).astype(BF)
-    ninth = jnp.where(within == 8, to_device, jnp.zeros_like(to_device))
     ninth_rows = dot(ninth, unit[...])
-    field = iota((DEVICES, ROWS), 0) >> 4
-    meta = jnp.where(field == 0, (local >> 8) + 1, jnp.where(field == 1, local & 255, jnp.where(field == 2, cid + 1, 0)))
-    meta = jnp.where(field == 3, rank >> 8, jnp.where(field == 4, rank & 255, meta))
-    meta = jnp.where((iota((DEVICES, ROWS), 0) & 15) == within, meta, 0).astype(F32).astype(BF)
-    extra[...] = jnp.zeros_like(extra)
     for part in range(6):
         extra[pl.ds(part, DEVICES, stride=8), :] = ninth_rows[:, part * 128 : (part + 1) * 128]
-    extra[pl.ds(6, DEVICES, stride=8), :] = dot_nt(to_device, meta)
     out_ref[:, ROWS:] = extra[...].astype(BF)
 
 

time: 91.5 us -> 91.6 us (level)
  no operation moved by 1% of the time
where the time goes in v6:
time: 91.6 us; the launch traced here: 91.4 us
  blocking collectives  60.3 us (66%)
  Pallas kernels  14.9 us (16%)
  waiting for transfers between devices  9.64 us (11%)
  starting transfers between devices  5.75 us (6%)
    all_to_all x1, blocking collectives, body(): got = lax.all_to_all(send, AXES, split_axis=0, concat_axis=0, tiled=True)  39 us
    all_to_all x1, blocking collectives, body(): lax.all_to_all(reply.reshape(DEVICES, 1, 128), AXES, split_axis=0, concat...  21.3 us
    pallas_call x7, Pallas kernels, call(): pl.pallas_call(kernel, out_shape=shapes if many else shapes[0], in_specs=...  14.9 us
    ppermute x1, waiting for transfers between devices, body(): mate = lax.ppermute(own, AXES, shift(-1))  9.64 us
    ppermute x1, starting transfers between devices, body(): key2 = lax.ppermute(own[EARLY:ROWS], AXES, shift(2))  2.91 us
    ppermute x1, starting transfers between devices, body(): key1 = lax.ppermute(first, AXES, shift(2))  2.5 us
  transfers between devices with their start and end apart: 4, of which 1 were waited for; matrix products, arithmetic and copies ran while one was open for 0% of the time, Pallas kernels for 6%

profile of v6, /device:TPU:1, one launch (start us, length us, event | category | flops | bytes accessed | tf_op | source)
XLA Modules:
  0.0 91.4 jit_solution(2732006797044577193)
XLA Ops:
  0.6 4.6 %pack.1 = (bf16[1024,896]{1,0:T(8,128)(2,1)}, s32[8,768]{1,0:T(8,128)}) custom-call(bf16[768,768]{1,0:T(8,128)(2,1)} %emb_ref.1, s32[768]{0:T(1024)} %cid_ref.1, s32[768]{0:T(1024)} %rank_ref.1, s32[768]{0:T(1024)} %slot_ref.1), custom_call_target="tpu_custom_call" | custom-call | bytes 1188864 | tf_op jit(solution)/shard_map/pack/pallas_call | solution.py:321
  5.3 39.0 %all_to_all.16 = bf16[128,8,896]{2,1,0:T(8,128)(2,1)S(1)} all-to-all(bf16[128,8,896]{2,1,0:T(8,128)(2,1)} %bitcast.9), channel_id=1, replica_groups=mesh['seg'=32,'pair'=4] {'seg','pair'}, dimensions={0} | all-to-all | bytes 3670016 | tf_op jit(solution)/shard_map/all_to_all | solution.py:351
  44.3 2.3 %unpack.1 = (bf16[784,768]{1,0:T(8,128)(2,1)S(1)}, bf16[528,768]{1,0:T(8,128)(2,1)S(1)}) custom-call(bf16[1024,896]{1,0:T(8,128)(2,1)S(1)} %bitcast.6), custom_call_target="tpu_custom_call" | custom-call | bytes 1835008 | tf_op jit(solution)/shard_map/unpack/pallas_call | solution.py:321
  46.6 0.3 collective-permute-start.1
  46.9 2.5 %collective-permute-start.2 = (bf16[528,768]{1,0:T(8,128)(2,1)S(1)}, bf16[528,768]{1,0:T(8,128)(2,1)S(1)}, u32[]{:S(2)}, u32[]{:S(2)}) collective-permute-start(bf16[528,768]{1,0:T(8,128)(2,1)S(1)} %get-tuple-element.8), channel_id=1, source_target_pairs={{87,83},{21,17},{91,87},{25,21},{107,91},{41,25},{111,107},{45,41}... | collective-permute-start | bytes 2433032 | tf_op jit(solution)/shard_map/ppermute | solution.py:360
  49.4 0.1 collective-permute-start.3
  49.6 2.9 %collective-permute-start = (bf16[256,768]{1,0:T(8,128)(2,1)S(1)}, bf16[256,768]{1,0:T(8,128)(2,1)S(1)}, u32[]{:S(2)}, u32[]{:S(2)}) collective-permute-start(bf16[256,768]{1,0:T(8,128)(2,1)S(1)} %slice.6), channel_id=1, source_target_pairs={{87,83},{21,17},{91,87},{25,21},{107,91},{41,25},{111,107},{45,41}... | collective-permute-start | bytes 1179656 | tf_op jit(solution)/shard_map/ppermute | solution.py:362
  52.5 1.4 %local.1.local_ref = f32[8,768]{1,0:T(8,128)S(1)} custom-call(bf16[784,768]{1,0:T(8,128)(2,1)S(1)} %get-tuple-element.7.own_ref), custom_call_target="tpu_custom_call" | custom-call | flops 905969664 | bytes 1204224 | tf_op jit(solution)/shard_map/local/pallas_call | solution.py:321
  53.9 9.6 %collective-permute-done.1.mate_ref = bf16[784,768]{1,0:T(8,128)(2,1)S(1)} collective-permute-done((bf16[784,768]{1,0:T(8,128)(2,1)S(1)}, bf16[784,768]{1,0:T(8,128)(2,1)S(1)}, u32[]{:S(2)}, u32[]{:S(2)}) %collective-permute-start.1) | collective-permute-done | bytes 1204256 | tf_op jit(solution)/shard_map/ppermute | solution.py:359
  63.5 1.5 %mate.1.near_ref = f32[8,768]{1,0:T(8,128)S(1)} custom-call(bf16[784,768]{1,0:T(8,128)(2,1)S(1)} %get-tuple-element.7.own_ref, bf16[784,768]{1,0:T(8,128)(2,1)S(1)} %collective-permute-done.1.mate_ref, f32[8,768]{1,0:T(8,128)S(1)} %local.1.local_ref), custom_call_target="tpu_custom_call" | custom-call | flops 905969664 | bytes 2433024 | tf_op jit(solution)/shard_map/mate/pallas_call | solution.py:321
  65.0 0.0 collective-permute-done.3.tail_ref
  65.0 0.0 collective-permute-done.2.key_ref.early_ref
  65.0 2.3 %far_first.1.first_ref = f32[8,768]{1,0:T(8,128)S(1)} custom-call(bf16[528,768]{1,0:T(8,128)(2,1)S(1)} %collective-permute-done.2.key_ref.early_ref, bf16[784,768]{1,0:T(8,128)(2,1)S(1)} %get-tuple-element.7.own_ref, bf16[784,768]{1,0:T(8,128)(2,1)S(1)} %collective-permute-done.1.mate_ref, bf16[400,768]{1,0:T(8,128)(2,1)S(1)} %collective-permute-done.3.tail_ref, ...), custom_call_target="tpu_custom_call" | custom-call | flops 905969664 | bytes 3858432 | tf_op jit(solution)/shard_map/far_first/pallas_call | solution.py:321
  67.3 0.0 copy-start
  67.3 0.0 collective-permute-done.key_ref
  67.4 1.8 %far_second.1 = f32[128,128]{1,0:T(8,128)S(1)} custom-call(bf16[256,768]{1,0:T(8,128)(2,1)S(1)} %collective-permute-done.key_ref, bf16[784,768]{1,0:T(8,128)(2,1)S(1)} %get-tuple-element.7.own_ref, bf16[784,768]{1,0:T(8,128)(2,1)S(1)} %collective-permute-done.1.mate_ref, bf16[528,768]{1,0:T(8,128)(2,1)S(1)} %collective-permute-done.2.key_ref.early_ref, ...), custom_call_target="tpu_custom_call" | custom-call | flops 905969664 | bytes 4251648 | tf_op jit(solution)/shard_map/far_second/pallas_call | solution.py:321
  69.2 21.3 %all_to_all.17 = f32[128,1,128]{2,1,0:T(1,128)S(1)} all-to-all(f32[128,1,128]{2,1,0:T(1,128)S(1)} %bitcast.7), channel_id=1, replica_groups=mesh['seg'=32,'pair'=4] {'seg','pair'}, dimensions={0} | all-to-all | bytes 131072 | tf_op jit(solution)/shard_map/all_to_all | solution.py:375
  90.4 0.0 copy-done
  90.4 0.9 %answer.1 = (f32[768]{0:T(1024)}, f32[768]{0:T(1024)}) custom-call(f32[128,128]{1,0:T(8,128)S(1)} %bitcast.8, s32[8,768]{1,0:T(8,128)S(1)} %copy-done), custom_call_target="tpu_custom_call" | custom-call | bytes 90112 | tf_op jit(solution)/shard_map/answer/pallas_call | solution.py:321
  (2 shorter events, 0.1 us)
Async XLA Ops:
  46.6 16.9 %collective-permute-start.1 = (bf16[784,768]{1,0:T(8,128)(2,1)S(1)}, bf16[784,768]{1,0:T(8,128)(2,1)S(1)}, u32[]{:S(2)}, u32[]{:S(2)}) collective-permute-start(bf16[784,768]{1,0:T(8,128)(2,1)S(1)} %get-tuple-element.7.own_ref), channel_id=1, source_target_pairs={{82,83},{83,17},{17,87},{87,21},{21,91},{91,25},{25,107},{107,41},... | collective-permute-start | bytes 3612680 | tf_op jit(solution)/shard_map/ppermute | solution.py:359
  46.9 18.1 %collective-permute-start.2 = (bf16[528,768]{1,0:T(8,128)(2,1)S(1)}, bf16[528,768]{1,0:T(8,128)(2,1)S(1)}, u32[]{:S(2)}, u32[]{:S(2)}) collective-permute-start(bf16[528,768]{1,0:T(8,128)(2,1)S(1)} %get-tuple-element.8), channel_id=1, source_target_pairs={{87,83},{21,17},{91,87},{25,21},{107,91},{41,25},{111,107},{45,41}... | collective-permute-start | bytes 2433032 | tf_op jit(solution)/shard_map/ppermute | solution.py:360
  49.4 15.6 %collective-permute-start.3 = (bf16[400,768]{1,0:T(8,128)(2,1)S(1)}, bf16[400,768]{1,0:T(8,128)(2,1)S(1)}, u32[]{:S(2)}, u32[]{:S(2)}) collective-permute-start(bf16[400,768]{1,0:T(8,128)(2,1)S(1)} %slice.7), channel_id=1, source_target_pairs={{18,83},{82,17},{83,87},{17,21},{87,91},{21,25},{91,107},{25,41},{... | collective-permute-start | bytes 1843208 | tf_op jit(solution)/shard_map/ppermute | solution.py:361
  49.6 17.8 %collective-permute-start = (bf16[256,768]{1,0:T(8,128)(2,1)S(1)}, bf16[256,768]{1,0:T(8,128)(2,1)S(1)}, u32[]{:S(2)}, u32[]{:S(2)}) collective-permute-start(bf16[256,768]{1,0:T(8,128)(2,1)S(1)} %slice.6), channel_id=1, source_target_pairs={{87,83},{21,17},{91,87},{25,21},{107,91},{41,25},{111,107},{45,41}... | collective-permute-start | bytes 1179656 | tf_op jit(solution)/shard_map/ppermute | solution.py:362
  67.3 23.1 %copy-start = (s32[8,768]{1,0:T(8,128)S(1)}, s32[8,768]{1,0:T(8,128)}, u32[]{:S(2)}) copy-start(s32[8,768]{1,0:T(8,128)} %get-tuple-element.9.route_ref) | copy-start | bytes 73732

commit v7 on v4

--- a/solution.py
+++ b/solution.py
@@ -78,10 +78,10 @@
 
 def pack_kernel(emb_ref, cid_ref, rank_ref, slot_ref, out_ref, route_ref, raw, slots, cids, ranks, unit, extra, sems):
     ids = ((slot_ref, slots), (cid_ref, cids), (rank_ref, ranks))
-    small = [pltpu.make_async_copy(*pair, sems.at[3 + i]) for i, pair in enumerate(ids)]
+    small = [pltpu.make_async_copy(*pair, sems.at[6 + i]) for i, pair in enumerate(ids)]
     copies = [
-        pltpu.make_async_copy(emb_ref.at[pl.ds(part * 256, 256)], raw.at[pl.ds(part * 256, 256)], sems.at[part])
-        for part in range(3)
+        pltpu.make_async_copy(emb_ref.at[pl.ds(part * 128, 128)], raw.at[pl.ds(part * 128, 128)], sems.at[part])
+        for part in range(6)
     ]
     for copy in small + copies:
         copy.start()
@@ -102,9 +102,9 @@
     flat = jnp.where(within < 8, device * 8 + within, -1)
     for part, copy in enumerate(copies):
         copy.wait()
-        values = raw[part * 256 : (part + 1) * 256, :].astype(F32)
+        values = raw[part * 128 : (part + 1) * 128, :].astype(F32)
         scaling = lax.rsqrt(jnp.sum(values * values, axis=1, keepdims=True) + 1e-06)
-        unit[part * 256 : (part + 1) * 256, :] = (values * scaling).astype(BF)
+        unit[part * 128 : (part + 1) * 128, :] = (values * scaling).astype(BF)
     for start in range(0, MAIN, 256):
         pick = (iota((256, ROWS), 0) + start == flat).astype(BF)
         out_ref[start : start + 256, :ROWS] = dot(pick, unit[...]).astype(BF)
@@ -342,7 +342,7 @@
             pltpu.VMEM((ROWS,), jnp.int32),
             pltpu.VMEM((ROWS, ROWS), BF),
             pltpu.VMEM((MAIN, 128), F32),
-            pltpu.SemaphoreType.DMA((6,)),
+            pltpu.SemaphoreType.DMA((9,)),
         ),
         name="pack",
         left=(0, 1, 2, 3),

time: 91.5 us -> 91.8 us (level)
  no operation moved by 1% of the time
where the time goes in v7:
time: 91.8 us; the launch traced here: 91.5 us
  blocking collectives  60.3 us (66%)
  Pallas kernels  15.1 us (16%)
  waiting for transfers between devices  9.63 us (10%)
  starting transfers between devices  5.75 us (6%)
    all_to_all x1, blocking collectives, body(): got = lax.all_to_all(send, AXES, split_axis=0, concat_axis=0, tiled=True)  39 us
    all_to_all x1, blocking collectives, body(): lax.all_to_all(reply.reshape(DEVICES, 1, 128), AXES, split_axis=0, concat...  21.3 us
    pallas_call x7, Pallas kernels, call(): pl.pallas_call(kernel, out_shape=shapes if many else shapes[0], in_specs=...  15.1 us
    ppermute x1, waiting for transfers between devices, body(): mate = lax.ppermute(own, AXES, shift(-1))  9.62 us
    ppermute x1, starting transfers between devices, body(): key2 = lax.ppermute(own[EARLY:ROWS], AXES, shift(2))  2.91 us
    ppermute x1, starting transfers between devices, body(): key1 = lax.ppermute(first, AXES, shift(2))  2.5 us
  transfers between devices with their start and end apart: 4, of which 1 were waited for; matrix products, arithmetic and copies ran while one was open for 0% of the time, Pallas kernels for 6%

profile of v7, /device:TPU:1, one launch (start us, length us, event | category | flops | bytes accessed | tf_op | source)
XLA Modules:
  0.0 91.5 jit_solution(7726926991207063153)
XLA Ops:
  0.6 4.8 %pack.1 = (bf16[1024,896]{1,0:T(8,128)(2,1)}, s32[8,768]{1,0:T(8,128)}) custom-call(bf16[768,768]{1,0:T(8,128)(2,1)} %emb_ref.1, s32[768]{0:T(1024)} %cid_ref.1, s32[768]{0:T(1024)} %rank_ref.1, s32[768]{0:T(1024)} %slot_ref.1), custom_call_target="tpu_custom_call" | custom-call | bytes 1188864 | tf_op jit(solution)/shard_map/pack/pallas_call | solution.py:321
  5.4 39.0 %all_to_all.16 = bf16[128,8,896]{2,1,0:T(8,128)(2,1)S(1)} all-to-all(bf16[128,8,896]{2,1,0:T(8,128)(2,1)} %bitcast.9), channel_id=1, replica_groups=mesh['seg'=32,'pair'=4] {'seg','pair'}, dimensions={0} | all-to-all | bytes 3670016 | tf_op jit(solution)/shard_map/all_to_all | solution.py:351
  44.4 2.3 %unpack.1 = (bf16[784,768]{1,0:T(8,128)(2,1)S(1)}, bf16[528,768]{1,0:T(8,128)(2,1)S(1)}) custom-call(bf16[1024,896]{1,0:T(8,128)(2,1)S(1)} %bitcast.6), custom_call_target="tpu_custom_call" | custom-call | bytes 1835008 | tf_op jit(solution)/shard_map/unpack/pallas_call | solution.py:321
  46.8 0.3 collective-permute-start.1
  47.0 2.5 %collective-permute-start.2 = (bf16[528,768]{1,0:T(8,128)(2,1)S(1)}, bf16[528,768]{1,0:T(8,128)(2,1)S(1)}, u32[]{:S(2)}, u32[]{:S(2)}) collective-permute-start(bf16[528,768]{1,0:T(8,128)(2,1)S(1)} %get-tuple-element.8), channel_id=1, source_target_pairs={{87,83},{21,17},{91,87},{25,21},{107,91},{41,25},{111,107},{45,41}... | collective-permute-start | bytes 2433032 | tf_op jit(solution)/shard_map/ppermute | solution.py:360
  49.6 0.1 collective-permute-start.3
  49.7 2.9 %collective-permute-start = (bf16[256,768]{1,0:T(8,128)(2,1)S(1)}, bf16[256,768]{1,0:T(8,128)(2,1)S(1)}, u32[]{:S(2)}, u32[]{:S(2)}) collective-permute-start(bf16[256,768]{1,0:T(8,128)(2,1)S(1)} %slice.6), channel_id=1, source_target_pairs={{87,83},{21,17},{91,87},{25,21},{107,91},{41,25},{111,107},{45,41}... | collective-permute-start | bytes 1179656 | tf_op jit(solution)/shard_map/ppermute | solution.py:362
  52.6 1.4 %local.1.local_ref = f32[8,768]{1,0:T(8,128)S(1)} custom-call(bf16[784,768]{1,0:T(8,128)(2,1)S(1)} %get-tuple-element.7.own_ref), custom_call_target="tpu_custom_call" | custom-call | flops 905969664 | bytes 1204224 | tf_op jit(solution)/shard_map/local/pallas_call | solution.py:321
  54.0 9.6 %collective-permute-done.1.mate_ref = bf16[784,768]{1,0:T(8,128)(2,1)S(1)} collective-permute-done((bf16[784,768]{1,0:T(8,128)(2,1)S(1)}, bf16[784,768]{1,0:T(8,128)(2,1)S(1)}, u32[]{:S(2)}, u32[]{:S(2)}) %collective-permute-start.1) | collective-permute-done | bytes 1204256 | tf_op jit(solution)/shard_map/ppermute | solution.py:359
  63.7 1.5 %mate.1.near_ref = f32[8,768]{1,0:T(8,128)S(1)} custom-call(bf16[784,768]{1,0:T(8,128)(2,1)S(1)} %get-tuple-element.7.own_ref, bf16[784,768]{1,0:T(8,128)(2,1)S(1)} %collective-permute-done.1.mate_ref, f32[8,768]{1,0:T(8,128)S(1)} %local.1.local_ref), custom_call_target="tpu_custom_call" | custom-call | flops 905969664 | bytes 2433024 | tf_op jit(solution)/shard_map/mate/pallas_call | solution.py:321
  65.2 0.0 collective-permute-done.3.tail_ref
  65.2 0.0 collective-permute-done.2.key_ref.early_ref
  65.2 2.3 %far_first.1.first_ref = f32[8,768]{1,0:T(8,128)S(1)} custom-call(bf16[528,768]{1,0:T(8,128)(2,1)S(1)} %collective-permute-done.2.key_ref.early_ref, bf16[784,768]{1,0:T(8,128)(2,1)S(1)} %get-tuple-element.7.own_ref, bf16[784,768]{1,0:T(8,128)(2,1)S(1)} %collective-permute-done.1.mate_ref, bf16[400,768]{1,0:T(8,128)(2,1)S(1)} %collective-permute-done.3.tail_ref, ...), custom_call_target="tpu_custom_call" | custom-call | flops 905969664 | bytes 3858432 | tf_op jit(solution)/shard_map/far_first/pallas_call | solution.py:321
  67.5 0.0 copy-start
  67.5 0.0 collective-permute-done.key_ref
  67.5 1.8 %far_second.1 = f32[128,128]{1,0:T(8,128)S(1)} custom-call(bf16[256,768]{1,0:T(8,128)(2,1)S(1)} %collective-permute-done.key_ref, bf16[784,768]{1,0:T(8,128)(2,1)S(1)} %get-tuple-element.7.own_ref, bf16[784,768]{1,0:T(8,128)(2,1)S(1)} %collective-permute-done.1.mate_ref, bf16[528,768]{1,0:T(8,128)(2,1)S(1)} %collective-permute-done.2.key_ref.early_ref, ...), custom_call_target="tpu_custom_call" | custom-call | flops 905969664 | bytes 4251648 | tf_op jit(solution)/shard_map/far_second/pallas_call | solution.py:321
  69.3 21.3 %all_to_all.17 = f32[128,1,128]{2,1,0:T(1,128)S(1)} all-to-all(f32[128,1,128]{2,1,0:T(1,128)S(1)} %bitcast.7), channel_id=1, replica_groups=mesh['seg'=32,'pair'=4] {'seg','pair'}, dimensions={0} | all-to-all | bytes 131072 | tf_op jit(solution)/shard_map/all_to_all | solution.py:375
  90.6 0.0 copy-done
  90.6 0.9 %answer.1 = (f32[768]{0:T(1024)}, f32[768]{0:T(1024)}) custom-call(f32[128,128]{1,0:T(8,128)S(1)} %bitcast.8, s32[8,768]{1,0:T(8,128)S(1)} %copy-done), custom_call_target="tpu_custom_call" | custom-call | bytes 90112 | tf_op jit(solution)/shard_map/answer/pallas_call | solution.py:321
  (2 shorter events, 0.1 us)
Async XLA Ops:
  46.8 16.9 %collective-permute-start.1 = (bf16[784,768]{1,0:T(8,128)(2,1)S(1)}, bf16[784,768]{1,0:T(8,128)(2,1)S(1)}, u32[]{:S(2)}, u32[]{:S(2)}) collective-permute-start(bf16[784,768]{1,0:T(8,128)(2,1)S(1)} %get-tuple-element.7.own_ref), channel_id=1, source_target_pairs={{82,83},{83,17},{17,87},{87,21},{21,91},{91,25},{25,107},{107,41},... | collective-permute-start | bytes 3612680 | tf_op jit(solution)/shard_map/ppermute | solution.py:359
  47.0 18.1 %collective-permute-start.2 = (bf16[528,768]{1,0:T(8,128)(2,1)S(1)}, bf16[528,768]{1,0:T(8,128)(2,1)S(1)}, u32[]{:S(2)}, u32[]{:S(2)}) collective-permute-start(bf16[528,768]{1,0:T(8,128)(2,1)S(1)} %get-tuple-element.8), channel_id=1, source_target_pairs={{87,83},{21,17},{91,87},{25,21},{107,91},{41,25},{111,107},{45,41}... | collective-permute-start | bytes 2433032 | tf_op jit(solution)/shard_map/ppermute | solution.py:360
  49.6 15.6 %collective-permute-start.3 = (bf16[400,768]{1,0:T(8,128)(2,1)S(1)}, bf16[400,768]{1,0:T(8,128)(2,1)S(1)}, u32[]{:S(2)}, u32[]{:S(2)}) collective-permute-start(bf16[400,768]{1,0:T(8,128)(2,1)S(1)} %slice.7), channel_id=1, source_target_pairs={{18,83},{82,17},{83,87},{17,21},{87,91},{21,25},{91,107},{25,41},{... | collective-permute-start | bytes 1843208 | tf_op jit(solution)/shard_map/ppermute | solution.py:361
  49.7 17.8 %collective-permute-start = (bf16[256,768]{1,0:T(8,128)(2,1)S(1)}, bf16[256,768]{1,0:T(8,128)(2,1)S(1)}, u32[]{:S(2)}, u32[]{:S(2)}) collective-permute-start(bf16[256,768]{1,0:T(8,128)(2,1)S(1)} %slice.6), channel_id=1, source_target_pairs={{87,83},{21,17},{91,87},{25,21},{107,91},{41,25},{111,107},{45,41}... | collective-permute-start | bytes 1179656 | tf_op jit(solution)/shard_map/ppermute | solution.py:362
  67.5 23.1 %copy-start = (s32[8,768]{1,0:T(8,128)S(1)}, s32[8,768]{1,0:T(8,128)}, u32[]{:S(2)}) copy-start(s32[8,768]{1,0:T(8,128)} %get-tuple-element.9.route_ref) | copy-start | bytes 73732

commit v8 on v4

--- a/solution.py
+++ b/solution.py
@@ -8,22 +8,22 @@
 AXES = ("seg", "pair")
 DEVICES = 128
 PLACES = [
-    (3, 0, 1, 1), (0, 0, 1, 1), (3, 1, 1, 1), (0, 1, 1, 1), (3, 2, 1, 1), (0, 2, 1, 1), (3, 2, 2, 1), (0, 2, 2, 1),
-    (3, 3, 2, 1), (0, 3, 2, 1), (3, 0, 2, 1), (0, 0, 2, 1), (3, 1, 2, 1), (0, 1, 2, 1), (3, 1, 3, 1), (0, 1, 3, 1),
-    (3, 2, 3, 1), (0, 2, 3, 1), (3, 3, 3, 1), (0, 3, 3, 1), (3, 0, 3, 1), (0, 0, 3, 1), (3, 0, 0, 1), (0, 0, 0, 1),
-    (3, 1, 0, 1), (0, 1, 0, 1), (3, 2, 0, 1), (0, 2, 0, 1), (3, 3, 0, 1), (0, 3, 0, 1), (3, 3, 1, 1), (0, 3, 1, 1),
-    (0, 3, 1, 0), (1, 3, 1, 0), (0, 2, 1, 0), (1, 2, 1, 0), (0, 2, 0, 0), (1, 2, 0, 0), (0, 2, 3, 0), (1, 2, 3, 0),
-    (0, 2, 2, 0), (1, 2, 2, 0), (0, 1, 2, 0), (1, 1, 2, 0), (0, 1, 1, 0), (1, 1, 1, 0), (0, 1, 0, 0), (1, 1, 0, 0),
-    (0, 1, 3, 0), (1, 1, 3, 0), (0, 0, 3, 0), (1, 0, 3, 0), (0, 0, 2, 0), (1, 0, 2, 0), (0, 0, 1, 0), (1, 0, 1, 0),
-    (0, 0, 0, 0), (1, 0, 0, 0), (0, 3, 0, 0), (1, 3, 0, 0), (0, 3, 3, 0), (1, 3, 3, 0), (0, 3, 2, 0), (1, 3, 2, 0),
-    (1, 3, 2, 1), (2, 3, 2, 1), (1, 2, 2, 1), (2, 2, 2, 1), (1, 2, 1, 1), (2, 2, 1, 1), (1, 1, 1, 1), (2, 1, 1, 1),
-    (1, 0, 1, 1), (2, 0, 1, 1), (1, 3, 1, 1), (2, 3, 1, 1), (1, 3, 0, 1), (2, 3, 0, 1), (1, 2, 0, 1), (2, 2, 0, 1),
-    (1, 1, 0, 1), (2, 1, 0, 1), (1, 0, 0, 1), (2, 0, 0, 1), (1, 0, 3, 1), (2, 0, 3, 1), (1, 3, 3, 1), (2, 3, 3, 1),
-    (1, 2, 3, 1), (2, 2, 3, 1), (1, 1, 3, 1), (2, 1, 3, 1), (1, 1, 2, 1), (2, 1, 2, 1), (1, 0, 2, 1), (2, 0, 2, 1),
-    (2, 0, 2, 0), (3, 0, 2, 0), (2, 0, 3, 0), (3, 0, 3, 0), (2, 1, 3, 0), (3, 1, 3, 0), (2, 1, 0, 0), (3, 1, 0, 0),
-    (2, 1, 1, 0), (3, 1, 1, 0), (2, 1, 2, 0), (3, 1, 2, 0), (2, 2, 2, 0), (3, 2, 2, 0), (2, 2, 3, 0), (3, 2, 3, 0),
-    (2, 2, 0, 0), (3, 2, 0, 0), (2, 2, 1, 0), (3, 2, 1, 0), (2, 3, 1, 0), (3, 3, 1, 0), (2, 3, 2, 0), (3, 3, 2, 0),
-    (2, 3, 3, 0), (3, 3, 3, 0), (2, 3, 0, 0), (3, 3, 0, 0), (2, 0, 0, 0), (3, 0, 0, 0), (2, 0, 1, 0), (3, 0, 1, 0),
+    (3, 0, 1, 0), (2, 0, 1, 0), (3, 0, 0, 0), (2, 0, 0, 0), (3, 3, 0, 0), (2, 3, 0, 0), (3, 3, 3, 0), (2, 3, 3, 0),
+    (3, 3, 2, 0), (2, 3, 2, 0), (3, 3, 1, 0), (2, 3, 1, 0), (3, 2, 1, 0), (2, 2, 1, 0), (3, 2, 0, 0), (2, 2, 0, 0),
+    (3, 2, 3, 0), (2, 2, 3, 0), (3, 2, 2, 0), (2, 2, 2, 0), (3, 1, 2, 0), (2, 1, 2, 0), (3, 1, 1, 0), (2, 1, 1, 0),
+    (3, 1, 0, 0), (2, 1, 0, 0), (3, 1, 3, 0), (2, 1, 3, 0), (3, 0, 3, 0), (2, 0, 3, 0), (3, 0, 2, 0), (2, 0, 2, 0),
+    (2, 0, 2, 1), (1, 0, 2, 1), (2, 1, 2, 1), (1, 1, 2, 1), (2, 1, 3, 1), (1, 1, 3, 1), (2, 2, 3, 1), (1, 2, 3, 1),
+    (2, 3, 3, 1), (1, 3, 3, 1), (2, 0, 3, 1), (1, 0, 3, 1), (2, 0, 0, 1), (1, 0, 0, 1), (2, 1, 0, 1), (1, 1, 0, 1),
+    (2, 2, 0, 1), (1, 2, 0, 1), (2, 3, 0, 1), (1, 3, 0, 1), (2, 3, 1, 1), (1, 3, 1, 1), (2, 0, 1, 1), (1, 0, 1, 1),
+    (2, 1, 1, 1), (1, 1, 1, 1), (2, 2, 1, 1), (1, 2, 1, 1), (2, 2, 2, 1), (1, 2, 2, 1), (2, 3, 2, 1), (1, 3, 2, 1),
+    (1, 3, 2, 0), (0, 3, 2, 0), (1, 3, 3, 0), (0, 3, 3, 0), (1, 3, 0, 0), (0, 3, 0, 0), (1, 0, 0, 0), (0, 0, 0, 0),
+    (1, 0, 1, 0), (0, 0, 1, 0), (1, 0, 2, 0), (0, 0, 2, 0), (1, 0, 3, 0), (0, 0, 3, 0), (1, 1, 3, 0), (0, 1, 3, 0),
+    (1, 1, 0, 0), (0, 1, 0, 0), (1, 1, 1, 0), (0, 1, 1, 0), (1, 1, 2, 0), (0, 1, 2, 0), (1, 2, 2, 0), (0, 2, 2, 0),
+    (1, 2, 3, 0), (0, 2, 3, 0), (1, 2, 0, 0), (0, 2, 0, 0), (1, 2, 1, 0), (0, 2, 1, 0), (1, 3, 1, 0), (0, 3, 1, 0),
+    (0, 3, 1, 1), (3, 3, 1, 1), (0, 3, 0, 1), (3, 3, 0, 1), (0, 2, 0, 1), (3, 2, 0, 1), (0, 1, 0, 1), (3, 1, 0, 1),
+    (0, 0, 0, 1), (3, 0, 0, 1), (0, 0, 3, 1), (3, 0, 3, 1), (0, 3, 3, 1), (3, 3, 3, 1), (0, 2, 3, 1), (3, 2, 3, 1),
+    (0, 1, 3, 1), (3, 1, 3, 1), (0, 1, 2, 1), (3, 1, 2, 1), (0, 0, 2, 1), (3, 0, 2, 1), (0, 3, 2, 1), (3, 3, 2, 1),
+    (0, 2, 2, 1), (3, 2, 2, 1), (0, 2, 1, 1), (3, 2, 1, 1), (0, 1, 1, 1), (3, 1, 1, 1), (0, 0, 1, 1), (3, 0, 1, 1),
 ]
 ROWS = 768
 HALF = 384

time: 91.5 us -> 91.5 us (level)
  waiting for transfers between devices: 9.62 us -> 16.3 us
  blocking collectives: 60.3 us -> 56.1 us
  starting transfers between devices: 5.75 us -> 3.38 us
    all_to_all x1, blocking collectives: 21.3 us -> 17.1 us  [body(): lax.all_to_all(reply.reshape(DEVICES, 1, 128), AXES, split_axis=0, concat...]
    ppermute x1, waiting for transfers between devices: 0.01 us -> 3.55 us  [body(): tail = lax.ppermute(own[HALF:], AXES, shift(-2))]
    ppermute x1, waiting for transfers between devices: 9.61 us -> 12.7 us  [body(): mate = lax.ppermute(own, AXES, shift(-1))]
    ppermute x1, starting transfers between devices: 2.91 us -> 0.26 us  [body(): key2 = lax.ppermute(own[EARLY:ROWS], AXES, shift(2))]
    ppermute x1, starting transfers between devices: 0.08 us -> 2.57 us  [body(): tail = lax.ppermute(own[HALF:], AXES, shift(-2))]
    ppermute x1, starting transfers between devices: 2.5 us -> 0.17 us  [body(): key1 = lax.ppermute(first, AXES, shift(2))]
  transfers between devices with their start and end apart: 4 -> 4, of which waited for: 1 -> 2; matrix products, arithmetic and copies ran while one was open for 0% -> 0% of each run, Pallas kernels for 6% -> 6%
where the time goes in v8:
time: 91.5 us; the launch traced here: 91.3 us
  blocking collectives  56.1 us (61%)
  waiting for transfers between devices  16.3 us (18%)
  Pallas kernels  14.8 us (16%)
  starting transfers between devices  3.38 us (4%)
    all_to_all x1, blocking collectives, body(): got = lax.all_to_all(send, AXES, split_axis=0, concat_axis=0, tiled=True)  39 us
    all_to_all x1, blocking collectives, body(): lax.all_to_all(reply.reshape(DEVICES, 1, 128), AXES, split_axis=0, concat...  17.1 us
    pallas_call x7, Pallas kernels, call(): pl.pallas_call(kernel, out_shape=shapes if many else shapes[0], in_specs=...  14.8 us
    ppermute x1, waiting for transfers between devices, body(): mate = lax.ppermute(own, AXES, shift(-1))  12.7 us
    ppermute x1, waiting for transfers between devices, body(): tail = lax.ppermute(own[HALF:], AXES, shift(-2))  3.55 us
    ppermute x1, starting transfers between devices, body(): tail = lax.ppermute(own[HALF:], AXES, shift(-2))  2.57 us
  transfers between devices with their start and end apart: 4, of which 2 were waited for; matrix products, arithmetic and copies ran while one was open for 0% of the time, Pallas kernels for 6%

profile of v8, /device:TPU:1, one launch (start us, length us, event | category | flops | bytes accessed | tf_op | source)
XLA Modules:
  0.0 91.3 jit_solution(7578821054989931996)
XLA Ops:
  0.6 4.5 %pack.1 = (bf16[1024,896]{1,0:T(8,128)(2,1)}, s32[8,768]{1,0:T(8,128)}) custom-call(bf16[768,768]{1,0:T(8,128)(2,1)} %emb_ref.1, s32[768]{0:T(1024)} %cid_ref.1, s32[768]{0:T(1024)} %rank_ref.1, s32[768]{0:T(1024)} %slot_ref.1), custom_call_target="tpu_custom_call" | custom-call | bytes 1188864 | tf_op jit(solution)/shard_map/pack/pallas_call | solution.py:321
  5.1 39.0 %all_to_all.16 = bf16[128,8,896]{2,1,0:T(8,128)(2,1)S(1)} all-to-all(bf16[128,8,896]{2,1,0:T(8,128)(2,1)} %bitcast.9), channel_id=1, replica_groups=mesh['seg'=32,'pair'=4] {'seg','pair'}, dimensions={0} | all-to-all | bytes 3670016 | tf_op jit(solution)/shard_map/all_to_all | solution.py:351
  44.1 2.3 %unpack.1 = (bf16[784,768]{1,0:T(8,128)(2,1)S(1)}, bf16[528,768]{1,0:T(8,128)(2,1)S(1)}) custom-call(bf16[1024,896]{1,0:T(8,128)(2,1)S(1)} %bitcast.6), custom_call_target="tpu_custom_call" | custom-call | bytes 1835008 | tf_op jit(solution)/shard_map/unpack/pallas_call | solution.py:321
  46.5 0.4 collective-permute-start.1
  46.8 0.2 collective-permute-start.2
  47.1 2.6 %collective-permute-start.3 = (bf16[400,768]{1,0:T(8,128)(2,1)S(1)}, bf16[400,768]{1,0:T(8,128)(2,1)S(1)}, u32[]{:S(2)}, u32[]{:S(2)}) collective-permute-start(bf16[400,768]{1,0:T(8,128)(2,1)S(1)} %slice.7), channel_id=1, source_target_pairs={{17,82},{83,18},{82,66},{18,2},{66,78},{2,14},{78,126},{14,62},{12... | collective-permute-start | bytes 1843208 | tf_op jit(solution)/shard_map/ppermute | solution.py:361
  49.7 0.3 collective-permute-start
  49.9 1.4 %local.1.local_ref = f32[8,768]{1,0:T(8,128)S(1)} custom-call(bf16[784,768]{1,0:T(8,128)(2,1)S(1)} %get-tuple-element.7.own_ref), custom_call_target="tpu_custom_call" | custom-call | flops 905969664 | bytes 1204224 | tf_op jit(solution)/shard_map/local/pallas_call | solution.py:321
  51.4 12.7 %collective-permute-done.1.mate_ref = bf16[784,768]{1,0:T(8,128)(2,1)S(1)} collective-permute-done((bf16[784,768]{1,0:T(8,128)(2,1)S(1)}, bf16[784,768]{1,0:T(8,128)(2,1)S(1)}, u32[]{:S(2)}, u32[]{:S(2)}) %collective-permute-start.1) | collective-permute-done | bytes 1204256 | tf_op jit(solution)/shard_map/ppermute | solution.py:359
  64.1 1.5 %mate.1.near_ref = f32[8,768]{1,0:T(8,128)S(1)} custom-call(bf16[784,768]{1,0:T(8,128)(2,1)S(1)} %get-tuple-element.7.own_ref, bf16[784,768]{1,0:T(8,128)(2,1)S(1)} %collective-permute-done.1.mate_ref, f32[8,768]{1,0:T(8,128)S(1)} %local.1.local_ref), custom_call_target="tpu_custom_call" | custom-call | flops 905969664 | bytes 2433024 | tf_op jit(solution)/shard_map/mate/pallas_call | solution.py:321
  65.6 3.5 %collective-permute-done.3.tail_ref = bf16[400,768]{1,0:T(8,128)(2,1)S(1)} collective-permute-done((bf16[400,768]{1,0:T(8,128)(2,1)S(1)}, bf16[400,768]{1,0:T(8,128)(2,1)S(1)}, u32[]{:S(2)}, u32[]{:S(2)}) %collective-permute-start.3) | collective-permute-done | bytes 614432 | tf_op jit(solution)/shard_map/ppermute | solution.py:361
  69.1 0.0 collective-permute-done.2.key_ref.early_ref
  69.1 2.3 %far_first.1.first_ref = f32[8,768]{1,0:T(8,128)S(1)} custom-call(bf16[528,768]{1,0:T(8,128)(2,1)S(1)} %collective-permute-done.2.key_ref.early_ref, bf16[784,768]{1,0:T(8,128)(2,1)S(1)} %get-tuple-element.7.own_ref, bf16[784,768]{1,0:T(8,128)(2,1)S(1)} %collective-permute-done.1.mate_ref, bf16[400,768]{1,0:T(8,128)(2,1)S(1)} %collective-permute-done.3.tail_ref, ...), custom_call_target="tpu_custom_call" | custom-call | flops 905969664 | bytes 3858432 | tf_op jit(solution)/shard_map/far_first/pallas_call | solution.py:321
  71.4 0.0 copy-start
  71.4 0.0 collective-permute-done.key_ref
  71.4 1.8 %far_second.1 = f32[128,128]{1,0:T(8,128)S(1)} custom-call(bf16[256,768]{1,0:T(8,128)(2,1)S(1)} %collective-permute-done.key_ref, bf16[784,768]{1,0:T(8,128)(2,1)S(1)} %get-tuple-element.7.own_ref, bf16[784,768]{1,0:T(8,128)(2,1)S(1)} %collective-permute-done.1.mate_ref, bf16[528,768]{1,0:T(8,128)(2,1)S(1)} %collective-permute-done.2.key_ref.early_ref, ...), custom_call_target="tpu_custom_call" | custom-call | flops 905969664 | bytes 4251648 | tf_op jit(solution)/shard_map/far_second/pallas_call | solution.py:321
  73.3 17.1 %all_to_all.17 = f32[128,1,128]{2,1,0:T(1,128)S(1)} all-to-all(f32[128,1,128]{2,1,0:T(1,128)S(1)} %bitcast.7), channel_id=1, replica_groups=mesh['seg'=32,'pair'=4] {'seg','pair'}, dimensions={0} | all-to-all | bytes 131072 | tf_op jit(solution)/shard_map/all_to_all | solution.py:375
  90.3 0.0 copy-done
  90.3 0.9 %answer.1 = (f32[768]{0:T(1024)}, f32[768]{0:T(1024)}) custom-call(f32[128,128]{1,0:T(8,128)S(1)} %bitcast.8, s32[8,768]{1,0:T(8,128)S(1)} %copy-done), custom_call_target="tpu_custom_call" | custom-call | bytes 90112 | tf_op jit(solution)/shard_map/answer/pallas_call | solution.py:321
  (2 shorter events, 0.1 us)
Async XLA Ops:
  46.5 17.6 %collective-permute-start.1 = (bf16[784,768]{1,0:T(8,128)(2,1)S(1)}, bf16[784,768]{1,0:T(8,128)(2,1)S(1)}, u32[]{:S(2)}, u32[]{:S(2)}) collective-permute-start(bf16[784,768]{1,0:T(8,128)(2,1)S(1)} %get-tuple-element.7.own_ref), channel_id=1, source_target_pairs={{83,82},{82,18},{18,66},{66,2},{2,78},{78,14},{14,126},{126,62},{6... | collective-permute-start | bytes 3612680 | tf_op jit(solution)/shard_map/ppermute | solution.py:359
  46.8 22.3 %collective-permute-start.2 = (bf16[528,768]{1,0:T(8,128)(2,1)S(1)}, bf16[528,768]{1,0:T(8,128)(2,1)S(1)}, u32[]{:S(2)}, u32[]{:S(2)}) collective-permute-start(bf16[528,768]{1,0:T(8,128)(2,1)S(1)} %get-tuple-element.8), channel_id=1, source_target_pairs={{66,82},{2,18},{78,66},{14,2},{126,78},{62,14},{110,126},{46,62},{... | collective-permute-start | bytes 2433032 | tf_op jit(solution)/shard_map/ppermute | solution.py:360
  47.1 22.1 %collective-permute-start.3 = (bf16[400,768]{1,0:T(8,128)(2,1)S(1)}, bf16[400,768]{1,0:T(8,128)(2,1)S(1)}, u32[]{:S(2)}, u32[]{:S(2)}) collective-permute-start(bf16[400,768]{1,0:T(8,128)(2,1)S(1)} %slice.7), channel_id=1, source_target_pairs={{17,82},{83,18},{82,66},{18,2},{66,78},{2,14},{78,126},{14,62},{12... | collective-permute-start | bytes 1843208 | tf_op jit(solution)/shard_map/ppermute | solution.py:361
  49.7 21.8 %collective-permute-start = (bf16[256,768]{1,0:T(8,128)(2,1)S(1)}, bf16[256,768]{1,0:T(8,128)(2,1)S(1)}, u32[]{:S(2)}, u32[]{:S(2)}) collective-permute-start(bf16[256,768]{1,0:T(8,128)(2,1)S(1)} %slice.6), channel_id=1, source_target_pairs={{66,82},{2,18},{78,66},{14,2},{126,78},{62,14},{110,126},{46,62},{... | collective-permute-start | bytes 1179656 | tf_op jit(solution)/shard_map/ppermute | solution.py:362
  71.4 18.9 %copy-start = (s32[8,768]{1,0:T(8,128)S(1)}, s32[8,768]{1,0:T(8,128)}, u32[]{:S(2)}) copy-start(s32[8,768]{1,0:T(8,128)} %get-tuple-element.9.route_ref) | copy-start | bytes 73732
